TPU v7x, 32 devices: a whole 2x2x4 slice. The times are simulated.
32 devices in a mesh: gz: 4 (over y, x), gy: 4 (over z), gx: 2 (over core).
Axes of the slice: x: 2, y: 2, z: 4, core: 2. Of those that a mesh axis runs over, the one named last changes fastest.
Arguments:
- section: bfloat16 [4, 1024, 512], P('gz', 'gy', 'gx'), may hold values from -6 to 6
- first_kernel: float32 [16, 9], replicated, may hold values from -2 to 2
- first_bias: float32 [16], replicated, may hold values from -3 to 3
- second_kernel: bfloat16 [9, 16, 16], replicated, may hold values from -0.5 to 0.5
- second_bias: float32 [16], replicated, may hold values from -3 to 3
- head_weight: float32 [16], replicated, may hold values from -1.5 to 1.5
Outputs:
- spectra: float32 [4, 2, 1024, 512], P('gz', None, 'gy', 'gx')
All inputs are finite; a program needn't handle non-finite values.
Results may differ from a plain program's by a relative error of at most 0.0075.
Values may be sent and summed in bfloat16 or wider, within the bound.
A program may use at most 128 MiB of HBM per device.

v0:
```python
import math

import jax
import jax.numpy as jnp
from jax import lax
from jax.sharding import PartitionSpec as P

PATCH = 128


def with_halo(cells, sides, width):
    for axis, dim in sides:
        count = lax.axis_size(axis)
        ends = count - 1
        head = lax.slice_in_dim(cells, 0, width, axis=dim)
        tail = lax.slice_in_dim(cells, cells.shape[dim] - width, cells.shape[dim], axis=dim)
        cells = jnp.concatenate(
            [
                lax.ppermute(tail, axis, [(i, (i + 1) % count) for i in range(ends)]),
                cells,
                lax.ppermute(head, axis, [((i + 1) % count, i) for i in range(ends)]),
            ],
            axis=dim,
        )
    return cells


def from_behind(value, axis, steps):
    count = lax.axis_size(axis)
    leading, last = (max(0, -steps), min(count, count - steps))
    return lax.ppermute(value, axis, [(source, source + steps) for source in range(leading, last)])


def dft_tables(length):
    positions = jnp.arange(length, dtype=jnp.int32)
    phase_step = positions[:, None] * positions[None, :] % length
    angles = phase_step.astype(jnp.float32) * (2.0 * math.pi / length)
    scaling = 1.0 / math.sqrt(length)
    cosine_table = (jnp.cos(angles) * scaling).astype(jnp.bfloat16)
    sine_table = (jnp.sin(angles) * scaling).astype(jnp.bfloat16)
    return (cosine_table, sine_table)


def first_layer(padded, kernel, offsets):
    row_count = padded.shape[0] - 2
    col_count = padded.shape[1] - 2
    values = padded.astype(jnp.float32)
    summed = jnp.zeros((kernel.shape[0], row_count, col_count), jnp.float32)
    for tap_index in range(9):
        row_off = tap_index // 3
        col_off = tap_index % 3
        window = values[row_off : row_off + row_count, col_off : col_off + col_count]
        summed = summed + kernel[:, tap_index][:, None, None] * window[None]
    return jax.nn.relu(summed + offsets[:, None, None]).astype(jnp.bfloat16)


def second_layer(hidden_pad, center, kernel, offsets, head_vec):
    row_count = hidden_pad.shape[1] - 2
    col_count = hidden_pad.shape[2] - 2
    summed = jnp.zeros((kernel.shape[1], row_count, col_count), jnp.float32)
    for tap_index in range(9):
        row_off = tap_index // 3
        col_off = tap_index % 3
        window = hidden_pad[:, row_off : row_off + row_count, col_off : col_off + col_count]
        summed = summed + jnp.einsum(
            "oc,crw->orw", kernel[tap_index], window, preferred_element_type=jnp.float32
        )
    deep = jax.nn.relu(summed + offsets[:, None, None])
    return (center.astype(jnp.float32) + jnp.sum(head_vec[:, None, None] * deep, axis=0)).astype(
        jnp.bfloat16
    )


def spectrum(restored, cosine_table, sine_table):
    length = cosine_table.shape[0]
    row_count, col_count = restored.shape
    tiles = restored.reshape(row_count // length, length, col_count // length, length)
    rows_cos = jnp.einsum(
        "aibj,jk->aibk", tiles, cosine_table, preferred_element_type=jnp.float32
    ).astype(jnp.bfloat16)
    rows_sin = jnp.einsum(
        "aibj,jk->aibk", tiles, sine_table, preferred_element_type=jnp.float32
    ).astype(jnp.bfloat16)
    real_part = jnp.einsum(
        "ij,aibk->ajbk", cosine_table, rows_cos, preferred_element_type=jnp.float32
    ) - jnp.einsum("ij,aibk->ajbk", sine_table, rows_sin, preferred_element_type=jnp.float32)
    imag_part = -(
        jnp.einsum("ij,aibk->ajbk", cosine_table, rows_sin, preferred_element_type=jnp.float32)
        + jnp.einsum("ij,aibk->ajbk", sine_table, rows_cos, preferred_element_type=jnp.float32)
    )
    return jnp.stack(
        [real_part.reshape(row_count, col_count), imag_part.reshape(row_count, col_count)]
    )


def cross(first_spec, second_spec):
    real_out = first_spec[0] * second_spec[0] + first_spec[1] * second_spec[1]
    imag_out = first_spec[1] * second_spec[0] - first_spec[0] * second_spec[1]
    return jnp.stack([real_out, imag_out])


def on_device(section, first_kernel, first_bias, second_kernel, second_bias, head_weight):
    section_image = section[0]
    padded = with_halo(section_image, (("gy", 0), ("gx", 1)), 1)
    hidden = first_layer(padded, first_kernel, first_bias)
    hidden_pad = with_halo(hidden, (("gy", 1), ("gx", 2)), 1)
    restored = second_layer(hidden_pad, section_image, second_kernel, second_bias, head_weight)
    cosine_table, sine_table = dft_tables(PATCH)
    own_spectrum = spectrum(restored, cosine_table, sine_table)
    upper_image = from_behind(restored, "gz", -1)
    next_spectra = spectrum(upper_image, cosine_table, sine_table)
    return cross(own_spectrum, next_spectra)[None]


def solution(mesh):
    placed = (P("gz", "gy", "gx"), P(), P(), P(), P(), P())
    return jax.shard_map(
        on_device, mesh=mesh, in_specs=placed, out_specs=P("gz", None, "gy", "gx"), check_vma=False
    )
```

profile of v0, /device:TPU:0, one launch (start us, length us, event | category | flops | bytes accessed | tf_op | source)
XLA Modules:
  0.0 94.7 jit_solution(2669179505140758217)
XLA Ops:
  0.7 4.9 %collective-permute-start = (bf16[1,256]{1,0:T(2,128)(2,1)S(1)}, bf16[1,256]{1,0:T(2,128)(2,1)S(1)}, u32[]{:S(2)}, u32[]{:S(2)}) collective-permute-start(bf16[1,256]{1,0:T(2,128)(2,1)S(1)} %get-tuple-element.33), channel_id=1, source_target_pairs={{0,2},{2,4},{4,6},{1,3},{3,5},{5,7},{8,10},{10,12},{12,14},{9,11},... | collective-permute-start | bytes 1544 | tf_op jit(solution)/shard_map/ppermute | solution.py:19
  7.0 4.2 %collective-permute-done.1 = bf16[1,256]{1,0:T(2,128)(2,1)S(1)} collective-permute-done((bf16[1,256]{1,0:T(2,128)(2,1)S(1)}, bf16[1,256]{1,0:T(2,128)(2,1)S(1)}, u32[]{:S(2)}, u32[]{:S(2)}) %collective-permute-start.1) | collective-permute-done | bytes 544 | tf_op jit(solution)/shard_map/ppermute | solution.py:21
  12.1 1.3 %collective-permute-start.2 = (bf16[258,1]{1,0:T(8,128)(2,1)S(1)}, bf16[258,1]{1,0:T(8,128)(2,1)S(1)}, u32[]{:S(2)}, u32[]{:S(2)}) collective-permute-start(bf16[258,1]{1,0:T(8,128)(2,1)S(1)} %get-tuple-element.31), channel_id=1, source_target_pairs={{0,1},{2,3},{4,5},{6,7},{8,9},{10,11},{12,13},{14,15},{16,17},{18,... | collective-permute-start | bytes 1556 | tf_op jit(solution)/shard_map/ppermute | solution.py:19
  14.7 1.4 %slice_reduce_fusion.8 = (f32[16]{0:T(128)S(1)}, f32[16]{0:T(128)S(1)}, f32[16]{0:T(128)S(1)}, f32[16]{0:T(128)S(1)}, f32[16]{0:T(128)S(1)}, /*index=5*/f32[16]{...) fusion(f32[16,9]{1,0:T(8,128)} %param.7), kind=kLoop, calls=%fused_computation.66 | loop fusion | bytes 1152 | tf_op jit(solution)/shard_map/slice | solution.py:53
  18.8 6.3 %maximum_convert_fusion = bf16[16,256,256]{2,0,1:T(8,128)(2,1)S(1)} fusion(f32[16]{0:T(128)S(1)} %copy-done.3, f32[256,256]{1,0:T(8,128)S(1)} %get-tuple-element.23, f32[16]{0:T(128)S(1)} %get-tuple-element.12, f32[256,256]{1,0:T(8,128)S(1)} %get-tuple-element.24, f32[16]{0:T(128)S(1)} %get-tuple-element.13, f32[256,256]{1,0:T(8,128)S(1)} %get-tuple-element.25, ...), kind=kLoop, calls=%fused_computation.1 | loop fusion | flops 20971520 | bytes 4457088 | tf_op jit(solution)/shard_map/convert_element_type | solution.py:54
  25.0 3.5 %collective-permute-start.4 = (bf16[16,1,256]{2,0,1:T(8,128)(2,1)S(1)}, bf16[16,1,256]{2,0,1:T(8,128)(2,1)S(1)}, u32[]{:S(2)}, u32[]{:S(2)}) collective-permute-start(bf16[16,1,256]{2,0,1:T(8,128)(2,1)S(1)} %get-tuple-element.18), channel_id=1, source_target_pairs={{0,2},{2,4},{4,6},{1,3},{3,5},{5,7},{8,10},{10,12},{12,14},{9,11},... | collective-permute-start | bytes 24584 | tf_op jit(solution)/shard_map/ppermute | solution.py:19
  29.8 2.6 %fusion.49 = f32[256,256,16]{1,2,0:T(8,128)} fusion(bf16[16,256,256]{2,0,1:T(8,128)(2,1)S(1)} %maximum_convert_fusion, bf16[9,16,16]{2,1,0:T(8,128)(2,1)S(1)} %copy-done.2), kind=kOutput, calls=%fused_computation.71 | convolution fusion | flops 33554432 | bytes 6295552 | tf_op jit(solution)/shard_map/oc,crw->orw/dot_general | solution.py:65
  32.5 1.6 %collective-permute-done.5 = bf16[16,1,256]{2,0,1:T(8,128)(2,1)S(1)} collective-permute-done((bf16[16,1,256]{2,0,1:T(8,128)(2,1)S(1)}, bf16[16,1,256]{2,0,1:T(8,128)(2,1)S(1)}, u32[]{:S(2)}, u32[]{:S(2)}) %collective-permute-start.5) | collective-permute-done | bytes 8224 | tf_op jit(solution)/shard_map/ppermute | solution.py:21
  34.4 1.5 %fusion.126 = (bf16[16,258,1]{2,0,1:T(8,128)(2,1)S(1)}, bf16[16,258,1]{2,0,1:T(8,128)(2,1)}) fusion(bf16[16,258,256]{2,0,1:T(8,128)(2,1)S(1)} %pad_maximum_fusion.1), kind=kLoop, calls=%fused_computation.150 | loop fusion | bytes 33024 | tf_op jit(solution)/shard_map/slice | solution.py:15
  35.8 2.1 %copy.31 = bf16[16,258,1]{1,0,2:T(8,128)(2,1)S(1)} copy(bf16[16,258,1]{2,0,1:T(8,128)(2,1)} %get-tuple-element.17) | data formatting | bytes 16512 | tf_op jit(solution)/shard_map/slice | solution.py:16
  38.0 1.6 %collective-permute-start.6 = (bf16[16,258,1]{1,0,2:T(8,128)(2,1)S(1)}, bf16[16,258,1]{1,0,2:T(8,128)(2,1)S(1)}, u32[]{:S(2)}, u32[]{:S(2)}) collective-permute-start(bf16[16,258,1]{1,0,2:T(8,128)(2,1)S(1)} %copy.31), channel_id=1, source_target_pairs={{0,1},{2,3},{4,5},{6,7},{8,9},{10,11},{12,13},{14,15},{16,17},{18,... | collective-permute-start | bytes 24776 | tf_op jit(solution)/shard_map/ppermute | solution.py:19
  40.6 1.5 %collective-permute-start.7 = (bf16[16,258,1]{1,0,2:T(8,128)(2,1)S(1)}, bf16[16,258,1]{1,0,2:T(8,128)(2,1)S(1)}, u32[]{:S(2)}, u32[]{:S(2)}) collective-permute-start(bf16[16,258,1]{1,0,2:T(8,128)(2,1)S(1)} %copy.33), channel_id=1, source_target_pairs={{1,0},{3,2},{5,4},{7,6},{9,8},{11,10},{13,12},{15,14},{17,16},{19,... | collective-permute-start | bytes 24776 | tf_op jit(solution)/shard_map/ppermute | solution.py:21
  42.1 2.7 %fusion.14 = f32[256,256,16]{1,2,0:T(8,128)} fusion(bf16[16,256,256]{2,0,1:T(8,128)(2,1)S(1)} %maximum_convert_fusion, bf16[16,1,256]{2,0,1:T(8,128)(2,1)S(1)} %collective-permute-done.4, bf16[9,16,16]{2,1,0:T(8,128)(2,1)S(1)} %copy-done.2), kind=kOutput, calls=%fused_computation.19 | convolution fusion | flops 37748736 | bytes 6303744 | tf_op jit(solution)/shard_map/oc,crw->orw/dot_general | solution.py:65
  44.8 2.6 %fusion.4 = f32[256,256,16]{1,2,0:T(8,128)} fusion(bf16[16,1,256]{2,0,1:T(8,128)(2,1)S(1)} %collective-permute-done.5, bf16[16,256,256]{2,0,1:T(8,128)(2,1)S(1)} %maximum_convert_fusion, bf16[9,16,16]{2,1,0:T(8,128)(2,1)S(1)} %copy-done.2), kind=kOutput, calls=%fused_computation.8 | convolution fusion | flops 37748736 | bytes 6303744 | tf_op jit(solution)/shard_map/oc,crw->orw/dot_general | solution.py:65
  48.6 2.2 %copy.34 = bf16[16,258,1]{2,0,1:T(8,128)(2,1)} copy(bf16[16,258,1]{1,0,2:T(8,128)(2,1)S(1)} %collective-permute-done.7) | data formatting | bytes 16512 | tf_op jit(solution)/shard_map/ppermute | solution.py:21
  50.8 5.0 %pad_maximum_fusion = (bf16[16,258,257]{2,0,1:T(8,128)(2,1)S(1)}, bf16[16,258,257]{2,0,1:T(8,128)(2,1)S(1)}) fusion(bf16[16,258,1]{2,0,1:T(8,128)(2,1)} %copy.34, bf16[16,1,256]{2,0,1:T(8,128)(2,1)S(1)} %collective-permute-done.5, bf16[16,256,256]{2,0,1:T(8,128)(2,1)S(1)} %maximum_convert_fusion, bf16[16,1,256]{2,0,1:T(8,128)(2,1)S(1)} %collective-permute-done.4, ...), kind=kLoop, calls=%fused_computation.3 | loop fusion | flops 16974336 | bytes 6373632 | tf_op jit(solution)/shard_map/concatenate | solution.py:17
  55.8 2.6 %fusion.10 = f32[256,256,16]{1,2,0:T(8,128)} fusion(bf16[16,258,257]{2,0,1:T(8,128)(2,1)S(1)} %get-tuple-element.15, bf16[9,16,16]{2,1,0:T(8,128)(2,1)S(1)} %copy-done.2), kind=kOutput, calls=%fused_computation.14 | convolution fusion | flops 33554432 | bytes 6295552 | tf_op jit(solution)/shard_map/oc,crw->orw/dot_general | solution.py:65
  58.4 2.6 %fusion.16 = f32[256,256,16]{1,2,0:T(8,128)} fusion(bf16[16,258,257]{2,0,1:T(8,128)(2,1)S(1)} %get-tuple-element.15, bf16[9,16,16]{2,1,0:T(8,128)(2,1)S(1)} %copy-done.2), kind=kOutput, calls=%fused_computation.21 | convolution fusion | flops 33554432 | bytes 6295552 | tf_op jit(solution)/shard_map/oc,crw->orw/dot_general | solution.py:65
  61.1 2.6 %fusion.6 = f32[256,256,16]{1,2,0:T(8,128)} fusion(bf16[16,258,257]{2,0,1:T(8,128)(2,1)S(1)} %get-tuple-element.15, bf16[9,16,16]{2,1,0:T(8,128)(2,1)S(1)} %copy-done.2), kind=kOutput, calls=%fused_computation.10 | convolution fusion | flops 33554432 | bytes 6295552 | tf_op jit(solution)/shard_map/oc,crw->orw/dot_general | solution.py:65
  63.7 2.8 %fusion.12 = f32[256,256,16]{1,2,0:T(8,128)} fusion(bf16[16,258,257]{2,0,1:T(8,128)(2,1)S(1)} %get-tuple-element.14, bf16[9,16,16]{2,1,0:T(8,128)(2,1)S(1)} %copy-done.2), kind=kOutput, calls=%fused_computation.16 | convolution fusion | flops 33554432 | bytes 6295552 | tf_op jit(solution)/shard_map/oc,crw->orw/dot_general | solution.py:65
  66.5 2.8 %fusion.8 = f32[256,256,16]{1,2,0:T(8,128)} fusion(bf16[16,258,257]{2,0,1:T(8,128)(2,1)S(1)} %get-tuple-element.14, bf16[9,16,16]{2,1,0:T(8,128)(2,1)S(1)} %copy-done.2), kind=kOutput, calls=%fused_computation.12 | convolution fusion | flops 33554432 | bytes 6295552 | tf_op jit(solution)/shard_map/oc,crw->orw/dot_general | solution.py:65
  69.7 11.0 %multiply_reduce_fusion = f32[256,256]{1,0:T(8,128)S(1)} fusion(f32[256,256,16]{1,2,0:T(8,128)} %fusion.4, f32[256,256,16]{1,2,0:T(8,128)} %fusion.6, f32[256,256,16]{1,2,0:T(8,128)} %fusion.8, f32[256,256,16]{1,2,0:T(8,128)S(1)} %copy-done, f32[256,256,16]{1,2,0:T(8,128)} %fusion.10, f32[256,256,16]{1,2,0:T(8,128)} %fusion.12, f32[256,256,16]{1,2,0:T(8,128)} %fusion.16, ...), kind=kOutput, calls=%fused_computation | convolution fusion | flops 46071808 | bytes 35918848 | tf_op jit(solution)/shard_map/oc,crw->orw/dot_general | solution.py:65
  81.9 1.5 %collective-permute-start.8 = (bf16[256,256]{1,0:T(8,128)(2,1)S(1)}, bf16[256,256]{1,0:T(8,128)(2,1)S(1)}, u32[]{:S(2)}, u32[]{:S(2)}) collective-permute-start(bf16[256,256]{1,0:T(8,128)(2,1)S(1)} %add_convert_fusion), channel_id=1, source_target_pairs={{8,0},{16,8},{24,16},{9,1},{17,9},{25,17},{10,2},{18,10},{26,18},{... | collective-permute-start | bytes 393224 | tf_op jit(solution)/shard_map/ppermute | solution.py:31
  84.7 5.3 %collective-permute-done.8 = bf16[256,256]{1,0:T(8,128)(2,1)S(1)} collective-permute-done((bf16[256,256]{1,0:T(8,128)(2,1)S(1)}, bf16[256,256]{1,0:T(8,128)(2,1)S(1)}, u32[]{:S(2)}, u32[]{:S(2)}) %collective-permute-start.8) | collective-permute-done | bytes 131104 | tf_op jit(solution)/shard_map/ppermute | solution.py:31
  (52 shorter events, 18.1 us)
Async XLA Ops:
  0.0 18.7 %copy-start.3 = (f32[16]{0:T(128)S(1)}, f32[16]{0:T(128)}, u32[]{:S(2)}) copy-start(f32[16]{0:T(128)} %param.8) | copy-start | bytes 196
  0.7 6.2 %collective-permute-start = (bf16[1,256]{1,0:T(2,128)(2,1)S(1)}, bf16[1,256]{1,0:T(2,128)(2,1)S(1)}, u32[]{:S(2)}, u32[]{:S(2)}) collective-permute-start(bf16[1,256]{1,0:T(2,128)(2,1)S(1)} %get-tuple-element.33), channel_id=1, source_target_pairs={{0,2},{2,4},{4,6},{1,3},{3,5},{5,7},{8,10},{10,12},{12,14},{9,11},... | collective-permute-start | bytes 1544 | tf_op jit(solution)/shard_map/ppermute | solution.py:19
  5.6 5.5 %collective-permute-start.1 = (bf16[1,256]{1,0:T(2,128)(2,1)S(1)}, bf16[1,256]{1,0:T(2,128)(2,1)S(1)}, u32[]{:S(2)}, u32[]{:S(2)}) collective-permute-start(bf16[1,256]{1,0:T(2,128)(2,1)S(1)} %get-tuple-element.34), channel_id=1, source_target_pairs={{2,0},{4,2},{6,4},{3,1},{5,3},{7,5},{10,8},{12,10},{14,12},{11,9},... | collective-permute-start | bytes 1544 | tf_op jit(solution)/shard_map/ppermute | solution.py:21
  12.1 5.0 %collective-permute-start.2 = (bf16[258,1]{1,0:T(8,128)(2,1)S(1)}, bf16[258,1]{1,0:T(8,128)(2,1)S(1)}, u32[]{:S(2)}, u32[]{:S(2)}) collective-permute-start(bf16[258,1]{1,0:T(8,128)(2,1)S(1)} %get-tuple-element.31), channel_id=1, source_target_pairs={{0,1},{2,3},{4,5},{6,7},{8,9},{10,11},{12,13},{14,15},{16,17},{18,... | collective-permute-start | bytes 1556 | tf_op jit(solution)/shard_map/ppermute | solution.py:19
  13.4 3.7 %collective-permute-start.3 = (bf16[258,1]{1,0:T(8,128)(2,1)S(1)}, bf16[258,1]{1,0:T(8,128)(2,1)S(1)}, u32[]{:S(2)}, u32[]{:S(2)}) collective-permute-start(bf16[258,1]{1,0:T(8,128)(2,1)S(1)} %get-tuple-element.32), channel_id=1, source_target_pairs={{1,0},{3,2},{5,4},{7,6},{9,8},{11,10},{13,12},{15,14},{17,16},{19,... | collective-permute-start | bytes 1556 | tf_op jit(solution)/shard_map/ppermute | solution.py:21
  18.3 11.6 %copy-start.2 = (bf16[9,16,16]{2,1,0:T(8,128)(2,1)S(1)}, bf16[9,16,16]{2,1,0:T(8,128)(2,1)}, u32[]{:S(2)}) copy-start(bf16[9,16,16]{2,1,0:T(8,128)(2,1)} %param.9) | copy-start | bytes 13828
  25.0 7.4 %collective-permute-start.4 = (bf16[16,1,256]{2,0,1:T(8,128)(2,1)S(1)}, bf16[16,1,256]{2,0,1:T(8,128)(2,1)S(1)}, u32[]{:S(2)}, u32[]{:S(2)}) collective-permute-start(bf16[16,1,256]{2,0,1:T(8,128)(2,1)S(1)} %get-tuple-element.18), channel_id=1, source_target_pairs={{0,2},{2,4},{4,6},{1,3},{3,5},{5,7},{8,10},{10,12},{12,14},{9,11},... | collective-permute-start | bytes 24584 | tf_op jit(solution)/shard_map/ppermute | solution.py:19
  28.5 5.5 %collective-permute-start.5 = (bf16[16,1,256]{2,0,1:T(8,128)(2,1)S(1)}, bf16[16,1,256]{2,0,1:T(8,128)(2,1)S(1)}, u32[]{:S(2)}, u32[]{:S(2)}) collective-permute-start(bf16[16,1,256]{2,0,1:T(8,128)(2,1)S(1)} %get-tuple-element.19), channel_id=1, source_target_pairs={{2,0},{4,2},{6,4},{3,1},{5,3},{7,5},{10,8},{12,10},{14,12},{11,9},... | collective-permute-start | bytes 24584 | tf_op jit(solution)/shard_map/ppermute | solution.py:21
  38.0 9.4 %collective-permute-start.6 = (bf16[16,258,1]{1,0,2:T(8,128)(2,1)S(1)}, bf16[16,258,1]{1,0,2:T(8,128)(2,1)S(1)}, u32[]{:S(2)}, u32[]{:S(2)}) collective-permute-start(bf16[16,258,1]{1,0,2:T(8,128)(2,1)S(1)} %copy.31), channel_id=1, source_target_pairs={{0,1},{2,3},{4,5},{6,7},{8,9},{10,11},{12,13},{14,15},{16,17},{18,... | collective-permute-start | bytes 24776 | tf_op jit(solution)/shard_map/ppermute | solution.py:19
  40.6 8.0 %collective-permute-start.7 = (bf16[16,258,1]{1,0,2:T(8,128)(2,1)S(1)}, bf16[16,258,1]{1,0,2:T(8,128)(2,1)S(1)}, u32[]{:S(2)}, u32[]{:S(2)}) collective-permute-start(bf16[16,258,1]{1,0,2:T(8,128)(2,1)S(1)} %copy.33), channel_id=1, source_target_pairs={{1,0},{3,2},{5,4},{7,6},{9,8},{11,10},{13,12},{15,14},{17,16},{19,... | collective-permute-start | bytes 24776 | tf_op jit(solution)/shard_map/ppermute | solution.py:21
  66.5 3.3 %copy-start = (f32[256,256,16]{1,2,0:T(8,128)S(1)}, f32[256,256,16]{1,2,0:T(8,128)}, u32[]{:S(2)}) copy-start(f32[256,256,16]{1,2,0:T(8,128)} %fusion.49) | copy-start | bytes 12582916
  66.5 3.3 %copy-start.4 = (f32[16]{0:T(128)S(1)}, f32[16]{0:T(128)}, u32[]{:S(2)}) copy-start(f32[16]{0:T(128)} %param.11) | copy-start | bytes 196
  66.5 3.3 %copy-start.5 = (f32[16]{0:T(128)S(1)}, f32[16]{0:T(128)}, u32[]{:S(2)}) copy-start(f32[16]{0:T(128)} %param.10) | copy-start | bytes 196
  69.7 11.0 %copy-start.1 = (bf16[1,256,256]{2,1,0:T(8,128)(2,1)S(1)}, bf16[1,256,256]{2,1,0:T(8,128)(2,1)}, u32[]{:S(2)}) copy-start(bf16[1,256,256]{2,1,0:T(8,128)(2,1)} %param.6) | copy-start | bytes 393220
  81.9 8.1 %collective-permute-start.8 = (bf16[256,256]{1,0:T(8,128)(2,1)S(1)}, bf16[256,256]{1,0:T(8,128)(2,1)S(1)}, u32[]{:S(2)}, u32[]{:S(2)}) collective-permute-start(bf16[256,256]{1,0:T(8,128)(2,1)S(1)} %add_convert_fusion), channel_id=1, source_target_pairs={{8,0},{16,8},{24,16},{9,1},{17,9},{25,17},{10,2},{18,10},{26,18},{... | collective-permute-start | bytes 393224 | tf_op jit(solution)/shard_map/ppermute | solution.py:31
where the time goes:
time: 95.2 us; the launch traced here: 94.7 us
  matrix products  37.5 us (39%)
  starting transfers between devices  18.1 us (19%)
  other arithmetic  14.5 us (15%)
  local copies, waits for them, and re-layouts  13.1 us (14%)
  waiting for transfers between devices  11.1 us (12%)
    dot_general x9, matrix products, second_layer(): jnp.einsum('oc,crw->orw', kernel[tap_index], window, preferred_element_ty...  32.4 us
    ppermute x4, starting transfers between devices, with_halo(): lax.ppermute(tail, axis, [(i, (i + 1) % count) for i in range(ends)])  11.3 us
    convert_element_type x1, other arithmetic, first_layer(): return jax.nn.relu(summed + offsets[:, None, None]).astype(jnp.bfloat16)  6.27 us
    concatenate x3, other arithmetic, with_halo(): jnp.concatenate([lax.ppermute(tail, axis, [(i, (i + 1) % count) for i in...  6.25 us
    ppermute x4, waiting for transfers between devices, with_halo(): lax.ppermute(head, axis, [((i + 1) % count, i) for i in range(ends)])  5.78 us
    ppermute x4, starting transfers between devices, with_halo(): lax.ppermute(head, axis, [((i + 1) % count, i) for i in range(ends)])  5.34 us
    ppermute x1, waiting for transfers between devices, from_behind(): lax.ppermute(value, axis, [(source, source + steps) for source in range(l...  5.32 us
    slice x4, local copies, waits for them, and re-layouts, with_halo(): lax.slice_in_dim(cells, cells.shape[dim] - width, cells.shape[dim], axis=...  2.96 us
  transfers between devices with their start and end apart: 9, of which 3 were waited for; matrix products, arithmetic and copies ran while one was open for 15% of the time, Pallas kernels for 0%

commit v1 on v0

v1 whole, which is shorter than its diff:
```python
import functools
import math

import jax
import jax.numpy as jnp
import numpy as np
from jax import lax
from jax.experimental import pallas as pl
from jax.experimental.pallas import tpu as pltpu
from jax.sharding import PartitionSpec as P

PATCH = 128
CH = 16
EDGE = 16
LANES = 128
ROWS_OUT = 8
F32 = jnp.float32
BF16 = jnp.bfloat16
MESH = pl.DeviceIdType.MESH
STEPS = [(-1, 0), (1, 0), (0, -1), (0, 1), (-1, -1), (-1, 1), (1, -1), (1, 1)]


def dft_table():
    positions = np.arange(PATCH)
    phase = (positions[:, None] * positions[None, :]) % PATCH
    angles = phase * (2.0 * math.pi / PATCH)
    both = np.concatenate([np.cos(angles), np.sin(angles)], axis=1) / math.sqrt(PATCH)
    return both.astype(np.float32).astype(jnp.bfloat16)


def iota(shape, dim):
    return lax.broadcasted_iota(jnp.int32, shape, dim)


def dot(a, b):
    return jnp.dot(a, b, preferred_element_type=F32)


def pieces(value, count):
    out = []
    for _ in range(count):
        part = value.astype(BF16)
        out.append(part)
        value = value - part.astype(F32)
    return out


def column_of(ref, ids):
    column = jnp.zeros(ids.shape, F32)
    for c in range(CH):
        column = jnp.where(ids == c, ref[c], column)
    return column


def first_weights(kernel_ref, bias_ref):
    rows, depth = 16 * CH, 256
    high, low = pieces(kernel_ref[...], 2)
    k = iota((9, depth), 1)
    tap = iota((9, depth), 0)
    split, col_off = k // 96, (k % 96) // 32
    m = iota((rows, depth), 0)
    kk = iota((rows, depth), 1)
    spread = jnp.where(iota((rows, CH), 0) % CH == iota((rows, CH), 1), 1.0, 0.0).astype(BF16)
    offset = (kk % 96) % 32 - 14 - m // CH
    weights = jnp.zeros((rows, depth), F32)
    for a in range(3):
        hit = tap == 3 * a + col_off
        placed = dot(high, jnp.where(hit & (split == 0), 1.0, 0.0).astype(BF16))
        placed = placed + dot(low, jnp.where(hit & (split == 1), 1.0, 0.0).astype(BF16))
        weights = jnp.where(offset == a, dot(spread, placed.astype(BF16)), weights)
    parts = pieces(column_of(bias_ref, m % CH), 3)
    weights = jnp.where(kk >= 192, 0.0, weights)
    for n, part in enumerate(parts):
        weights = jnp.where(kk == 192 + n, part.astype(F32), weights)
    return weights.astype(BF16)


def second_weights(kernel_ref, bias_ref):
    rows, depth = ROWS_OUT * CH, 512
    flat = kernel_ref[...].reshape(9 * CH, CH)
    tile = jnp.where(iota((CH, depth), 1) % CH == iota((CH, depth), 0), 1.0, 0.0).astype(BF16)
    tiled = dot(flat, tile).astype(BF16)
    spread = jnp.where(iota((rows, CH), 0) // ROWS_OUT == iota((rows, CH), 1), 1.0, 0.0).astype(BF16)
    m = iota((rows, depth), 0)
    kk = iota((rows, depth), 1)
    slot = kk // CH - 3 * (m % ROWS_OUT)
    weights = jnp.zeros((rows, depth), F32)
    for t in range(9):
        weights = jnp.where(slot == t, dot(spread, tiled[t * CH : (t + 1) * CH]), weights)
    parts = pieces(column_of(bias_ref, m // ROWS_OUT), 3)
    weights = jnp.where(kk >= 480, 0.0, weights)
    for n, part in enumerate(parts):
        weights = jnp.where(kk == 480 + n, part.astype(F32), weights)
    return weights.astype(BF16)


def spectrum(image, table):
    cosine, sine = table[:, :PATCH], table[:, PATCH:]
    patches = image.shape[1] // PATCH
    stacked = jnp.concatenate([image[:, n * PATCH : (n + 1) * PATCH] for n in range(patches)], axis=0)
    rows = dot(stacked, table).astype(BF16)
    parts = [rows[n * PATCH : (n + 1) * PATCH] for n in range(patches)]
    lower = jnp.concatenate(
        [
            jnp.concatenate([p[:, :PATCH] for p in parts], axis=1),
            jnp.concatenate([p[:, PATCH:] for p in parts], axis=1),
        ],
        axis=0,
    )
    full = jnp.concatenate(
        [jnp.concatenate([cosine, -sine], axis=1), jnp.concatenate([-sine, -cosine], axis=1)], axis=0
    )
    both = dot(full, lower)
    return both[:PATCH], both[PATCH:]


def body(
    sizes,
    x_ref, k1_ref, k2_ref, table_ref, b1_ref, b2_ref, hw_ref,
    out_ref,
    halo, shifted, hidden, own, following, w1_ref, w2_ref,
    halo_send, halo_recv, next_send, next_recv,
):
    n_gz, n_gy, n_gx = sizes
    height, width = x_ref.shape
    wide = width + LANES
    gz, gy, gx = lax.axis_index("gz"), lax.axis_index("gy"), lax.axis_index("gx")

    def present(dy, dx):
        y, x = gy + dy, gx + dx
        return (y >= 0) & (y < n_gy) & (x >= 0) & (x < n_gx)

    def device(dz, dy, dx):
        return (
            lax.rem(gz + dz + n_gz, n_gz),
            lax.rem(gy + dy + n_gy, n_gy),
            lax.rem(gx + dx + n_gx, n_gx),
        )

    not_first, not_last = gz > 0, gz < n_gz - 1

    barrier = pltpu.get_barrier_semaphore()
    count = not_first.astype(jnp.int32) + not_last.astype(jnp.int32)
    for dy, dx in STEPS:
        count = count + present(dy, dx).astype(jnp.int32)

        @pl.when(present(dy, dx))
        def _():
            pl.semaphore_signal(barrier, inc=1, device_id=device(0, dy, dx), device_id_type=MESH)

    @pl.when(not_first)
    def _():
        pl.semaphore_signal(barrier, inc=1, device_id=device(-1, 0, 0), device_id_type=MESH)

    @pl.when(not_last)
    def _():
        pl.semaphore_signal(barrier, inc=1, device_id=device(1, 0, 0), device_id_type=MESH)

    pl.semaphore_wait(barrier, count)

    row_src = {-1: (0, EDGE), 1: (height - EDGE, EDGE), 0: (0, height)}
    col_src = {-1: (0, LANES), 1: (width - LANES, LANES), 0: (0, width)}
    row_dst = {-1: EDGE + height, 1: 0, 0: EDGE}
    col_dst = {-1: width, 1: width + LANES, 0: 0}
    copies = []
    for n, (dy, dx) in enumerate(STEPS):
        (r0, rn), (c0, cn) = row_src[dy], col_src[dx]
        copies.append(
            pltpu.make_async_remote_copy(
                src_ref=x_ref.at[pl.ds(r0, rn), pl.ds(c0, cn)],
                dst_ref=halo.at[pl.ds(row_dst[dy], rn), pl.ds(col_dst[dx], cn)],
                send_sem=halo_send.at[n],
                recv_sem=halo_recv.at[n],
                device_id=device(0, dy, dx),
                device_id_type=MESH,
            )
        )
    for n, (dy, dx) in enumerate(STEPS):

        @pl.when(present(dy, dx))
        def _():
            copies[n].start()

        @pl.when(jnp.logical_not(present(-dy, -dx)))
        def _():
            rn, cn = row_src[dy][1], col_src[dx][1]
            halo[pl.ds(row_dst[dy], rn), pl.ds(col_dst[dx], cn)] = jnp.zeros((rn, cn), BF16)

    w1_ref[...] = first_weights(k1_ref, b1_ref)
    w2_ref[...] = second_weights(k2_ref, b2_ref)

    for n, (dy, dx) in enumerate(STEPS):

        @pl.when(present(-dy, -dx))
        def _():
            copies[n].wait_recv()

    def place(row, size, centre):
        right = halo[pl.ds(row, size), pl.ds(width, LANES)].astype(F32)
        left = halo[pl.ds(row, size), pl.ds(width + LANES, LANES)].astype(F32)
        side = jnp.where(iota((size, LANES), 1) < LANES // 2, right, left)
        ring = jnp.concatenate([centre.astype(F32), side], axis=1)
        shifted[0, pl.ds(row, size), :] = pltpu.roll(ring, 1, 1).astype(BF16)
        shifted[1, pl.ds(row, size), :] = ring.astype(BF16)
        shifted[2, pl.ds(row, size), :] = pltpu.roll(ring, wide - 1, 1).astype(BF16)

    place(0, EDGE, halo[0:EDGE, 0:width])
    place(EDGE + height, EDGE, halo[EDGE + height : 2 * EDGE + height, 0:width])

    def fill(i, carry):
        place(EDGE + i * 64, 64, x_ref[pl.ds(pl.multiple_of(i * 64, 64), 64), :])
        return carry

    lax.fori_loop(0, height // 64, fill, 0)

    lane = iota((1, wide), 1)
    keep = (lane < width) | ((lane == width) & (gx < n_gx - 1)) | ((lane == wide - 1) & (gx > 0))
    keep = jnp.where(keep, 1.0, 0.0)

    def layer_one(i, rows):
        start = pl.multiple_of(i * 16, 16)
        taps = [shifted[b, pl.ds(start, 32), :] for b in range(3)]
        stack = jnp.concatenate(taps + taps + [jnp.ones((16, wide), BF16)], axis=0)
        value = dot(w1_ref[0 : rows * CH, 0:208], stack)
        value = jnp.maximum(value, 0.0) * keep
        hidden[pl.ds(start, rows), CH : 2 * CH, :] = (
            value[:, :width].astype(BF16).reshape(rows, CH, width)
        )
        hidden[pl.ds(start, rows), 0:CH, :] = (
            pltpu.roll(value, 1, 1)[:, :width].astype(BF16).reshape(rows, CH, width)
        )
        hidden[pl.ds(start, rows), 2 * CH : 3 * CH, :] = (
            pltpu.roll(value, wide - 1, 1)[:, :width].astype(BF16).reshape(rows, CH, width)
        )

    def layer_two(i):
        start = pl.multiple_of(i * 16, 16)
        rows = []
        for g in range(2):
            window = hidden[pl.ds(start + g * ROWS_OUT, ROWS_OUT + 2), :, :].reshape(480, width)
            stack = jnp.concatenate([window, jnp.ones((16, width), BF16)], axis=0)
            deep = jnp.maximum(dot(w2_ref[:, 0:496], stack), 0.0)
            total = hw_ref[0] * deep[0:ROWS_OUT]
            for o in range(1, CH):
                total = total + hw_ref[o] * deep[o * ROWS_OUT : (o + 1) * ROWS_OUT]
            rows.append(total)
        total = jnp.concatenate(rows, axis=0)
        centre = x_ref[pl.ds(start, 16), :].astype(F32)
        own[pl.ds(start, 16), :] = (centre + total).astype(BF16)

    def one(i, carry):
        layer_one(i, 16)
        return carry

    def two(i, carry):
        layer_two(i)
        return carry

    bands = height // PATCH
    per_band = PATCH // 16
    blocks = height // 16
    sends = []
    done = 0
    for band in range(bands):
        upto = min((band + 1) * per_band + 1, blocks)
        lax.fori_loop(done, upto, one, 0)
        done = upto
        if band == 0:

            @pl.when(gy == 0)
            def _():
                hidden[0, :, :] = jnp.zeros((3 * CH, width), BF16)

        if band == bands - 1:
            layer_one(blocks, 2)

            @pl.when(gy == n_gy - 1)
            def _():
                hidden[height + 1, :, :] = jnp.zeros((3 * CH, width), BF16)

        lax.fori_loop(band * per_band, (band + 1) * per_band, two, 0)
        sends.append(
            pltpu.make_async_remote_copy(
                src_ref=own.at[pl.ds(band * PATCH, PATCH), :],
                dst_ref=following.at[pl.ds(band * PATCH, PATCH), :],
                send_sem=next_send.at[band],
                recv_sem=next_recv.at[band],
                device_id=device(-1, 0, 0),
                device_id_type=MESH,
            )
        )

        @pl.when(not_first)
        def _():
            sends[band].start()

    @pl.when(not_last)
    def _():
        table = table_ref[...]
        spectra = [spectrum(own[band * PATCH : (band + 1) * PATCH, :], table) for band in range(bands)]
        for band in range(bands):
            sends[band].wait_recv()
            real, imag = spectra[band]
            other_real, other_imag = spectrum(following[band * PATCH : (band + 1) * PATCH, :], table)
            rows = slice(band * PATCH, (band + 1) * PATCH)
            out_ref[0, 0, rows, :] = real * other_real + imag * other_imag
            out_ref[0, 1, rows, :] = imag * other_real - real * other_imag

    @pl.when(jnp.logical_not(not_last))
    def _():
        out_ref[...] = jnp.zeros(out_ref.shape, F32)

    for n, (dy, dx) in enumerate(STEPS):

        @pl.when(present(dy, dx))
        def _():
            copies[n].wait_send()

    @pl.when(not_first)
    def _():
        for band in range(bands):
            sends[band].wait_send()


def on_device(sizes, section, first_kernel, first_bias, second_kernel, second_bias, head_weight):
    height, width = section.shape[1:]
    bands = height // PATCH
    vmem = pl.BlockSpec(memory_space=pltpu.VMEM)
    smem = pl.BlockSpec(memory_space=pltpu.SMEM)
    return pl.pallas_call(
        functools.partial(body, sizes),
        out_shape=jax.ShapeDtypeStruct((1, 2, height, width), F32),
        in_specs=[vmem] * 4 + [smem] * 3,
        out_specs=vmem,
        scratch_shapes=[
            pltpu.VMEM((height + 2 * EDGE, width + 2 * LANES), BF16),
            pltpu.VMEM((3, height + 2 * EDGE, width + LANES), BF16),
            pltpu.VMEM((height + 16, 3 * CH, width), BF16),
            pltpu.VMEM((height, width), BF16),
            pltpu.VMEM((height, width), BF16),
            pltpu.VMEM((16 * CH, 256), BF16),
            pltpu.VMEM((ROWS_OUT * CH, 512), BF16),
            pltpu.SemaphoreType.DMA((8,)),
            pltpu.SemaphoreType.DMA((8,)),
            pltpu.SemaphoreType.DMA((bands,)),
            pltpu.SemaphoreType.DMA((bands,)),
        ],
        compiler_params=pltpu.CompilerParams(
            collective_id=0, has_side_effects=True, vmem_limit_bytes=48 * 1024 * 1024
        ),
        name="restore_spectra",
    )(section[0], first_kernel, second_kernel, jnp.asarray(dft_table()), first_bias, second_bias, head_weight)


def solution(mesh):
    sizes = tuple(mesh.shape[name] for name in ("gz", "gy", "gx"))
    placed = (P("gz", "gy", "gx"), P(), P(), P(), P(), P())
    return jax.shard_map(
        functools.partial(on_device, sizes),
        mesh=mesh,
        in_specs=placed,
        out_specs=P("gz", None, "gy", "gx"),
        check_vma=False,
    )
```

time: 95.2 us -> 26.1 us (0.27)
  matrix products: 37.5 us -> 0 us
  Pallas kernels: 0 us -> 21.1 us
  starting transfers between devices: 18.1 us -> 0 us
  other arithmetic: 14.5 us -> 0 us
  waiting for transfers between devices: 11.1 us -> 0 us
  local copies, waits for them, and re-layouts: 13.1 us -> 4.69 us
    dot_general x21 -> x0, matrix products: 37.5 us -> none  [the longest x9 32.4 us: second_layer(): jnp.einsum('oc,crw->orw', kernel[tap_index], window, preferred_element_ty...]
    pallas_call x0 -> x1, Pallas kernels: none -> 21.1 us  [on_device(): pl.pallas_call(functools.partial(body, sizes), out_shape=jax.ShapeDtypeSt...]
    ppermute x9 -> x0, starting transfers between devices: 18.1 us -> none  [the longest x4 11.3 us: with_halo(): lax.ppermute(tail, axis, [(i, (i + 1) % count) for i in range(ends)])]
    ppermute x9 -> x0, waiting for transfers between devices: 11.1 us -> none  [the longest x4 5.78 us: with_halo(): lax.ppermute(head, axis, [((i + 1) % count, i) for i in range(ends)])]
    convert_element_type x4 -> x0, other arithmetic: 7.41 us -> none  [the longest x1 6.27 us: first_layer(): return jax.nn.relu(summed + offsets[:, None, None]).astype(jnp.bfloat16)]
    slice x8 -> x0, local copies, waits for them, and re-layouts: 7.33 us -> none  [the longest x4 2.96 us: with_halo(): lax.slice_in_dim(cells, cells.shape[dim] - width, cells.shape[dim], axis=...]
    concatenate x3 -> x0, other arithmetic: 6.25 us -> none  [with_halo(): jnp.concatenate([lax.ppermute(tail, axis, [(i, (i + 1) % count) for i in...]
    unnamed x12 -> x15, local copies, waits for them, and re-layouts: 0.5 us -> 4.69 us
  transfers between devices with their start and end apart: 9 -> 0, of which waited for: 3 -> 0; matrix products, arithmetic and copies ran while one was open for 15% -> 0% of each run, Pallas kernels for 0% -> 0%
where the time goes in v1:
time: 26.1 us; the launch traced here: 25.8 us
  Pallas kernels  21.1 us (81%)
  local copies, waits for them, and re-layouts  4.69 us (18%)
    pallas_call x1, Pallas kernels, on_device(): pl.pallas_call(functools.partial(body, sizes), out_shape=jax.ShapeDtypeSt...  21.1 us
    unnamed x15, local copies, waits for them, and re-layouts  4.69 us

profile of v1, /device:TPU:0, one launch (start us, length us, event | category | flops | bytes accessed | tf_op | source)
XLA Modules:
  0.0 25.8 jit_solution(12587069941099879089)
XLA Ops:
  0.0 0.0 copy-start.6
  0.0 0.0 copy-start.5
  0.0 0.0 copy-start.4
  0.0 0.6 %copy-done.6 = f32[16]{0:T(128)S(1)} copy-done((f32[16]{0:T(128)S(1)}, f32[16]{0:T(128)}, u32[]{:S(2)}) %copy-start.6) | copy-done | bytes 88
  0.7 0.0 copy-done.5
  0.7 0.0 copy-done.4
  0.7 0.0 copy-start
  0.7 0.9 %copy-done = bf16[1,256,256]{2,1,0:T(8,128)(2,1)S(1)} copy-done((bf16[1,256,256]{2,1,0:T(8,128)(2,1)S(1)}, bf16[1,256,256]{2,1,0:T(8,128)(2,1)}, u32[]{:S(2)}) %copy-start) | copy-done | bytes 131096
  1.6 0.0 copy-start.1
  1.6 0.8 %copy-done.1 = bf16[128,256]{1,0:T(8,128)(2,1)S(1)} copy-done((bf16[128,256]{1,0:T(8,128)(2,1)S(1)}, bf16[128,256]{1,0:T(8,128)(2,1)}, u32[]{:S(2)}) %copy-start.1) | copy-done | bytes 65560
  2.4 0.0 copy-start.2
  2.4 0.8 %copy-done.2 = bf16[9,16,16]{2,1,0:T(8,128)(2,1)S(1)} copy-done((bf16[9,16,16]{2,1,0:T(8,128)(2,1)S(1)}, bf16[9,16,16]{2,1,0:T(8,128)(2,1)}, u32[]{:S(2)}) %copy-start.2) | copy-done | bytes 4632
  3.2 0.0 copy-start.3
  3.2 0.7 %copy-done.3 = f32[16,9]{1,0:T(8,128)S(1)} copy-done((f32[16,9]{1,0:T(8,128)S(1)}, f32[16,9]{1,0:T(8,128)}, u32[]{:S(2)}) %copy-start.3) | copy-done | bytes 600
  3.9 21.1 %restore_spectra.1 = f32[1,2,256,256]{3,2,1,0:T(8,128)S(1)} custom-call(bf16[256,256]{1,0:T(8,128)(2,1)S(1)} %bitcast.1, f32[16,9]{1,0:T(8,128)S(1)} %copy-done.3, bf16[9,16,16]{2,1,0:T(8,128)(2,1)S(1)} %copy-done.2, bf16[128,256]{1,0:T(8,128)(2,1)S(1)} %copy-done.1, f32[16]{0:T(128)S(1)} %copy-done.4, f32[16]{0:T(128)S(1)} %copy-done.5, f32[16]{0:T(128)S(1)} %copy-done.6), custom_call_target="tpu_custom_call" | custom-call | tf_op jit(solution)/shard_map/restore_spectra/pallas_call | solution.py:330
  25.0 0.8 %copy.9 = f32[1,2,256,256]{3,2,1,0:T(8,128)} copy(f32[1,2,256,256]{3,2,1,0:T(8,128)S(1)} %restore_spectra.1) | data formatting | bytes 1048576
Async XLA Ops:
  0.0 0.7 %copy-start.6 = (f32[16]{0:T(128)S(1)}, f32[16]{0:T(128)}, u32[]{:S(2)}) copy-start(f32[16]{0:T(128)} %hw_ref.1) | copy-start | bytes 196
  0.0 0.7 %copy-start.5 = (f32[16]{0:T(128)S(1)}, f32[16]{0:T(128)}, u32[]{:S(2)}) copy-start(f32[16]{0:T(128)} %b2_ref.1) | copy-start | bytes 196
  0.0 0.7 %copy-start.4 = (f32[16]{0:T(128)S(1)}, f32[16]{0:T(128)}, u32[]{:S(2)}) copy-start(f32[16]{0:T(128)} %b1_ref.1) | copy-start | bytes 196
  0.7 0.9 %copy-start = (bf16[1,256,256]{2,1,0:T(8,128)(2,1)S(1)}, bf16[1,256,256]{2,1,0:T(8,128)(2,1)}, u32[]{:S(2)}) copy-start(bf16[1,256,256]{2,1,0:T(8,128)(2,1)} %param.7) | copy-start | bytes 393220
  1.6 0.8 %copy-start.1 = (bf16[128,256]{1,0:T(8,128)(2,1)S(1)}, bf16[128,256]{1,0:T(8,128)(2,1)}, u32[]{:S(2)}) copy-start(bf16[128,256]{1,0:T(8,128)(2,1)} %constant.2.clone.table_ref) | copy-start | bytes 196612
  2.4 0.8 %copy-start.2 = (bf16[9,16,16]{2,1,0:T(8,128)(2,1)S(1)}, bf16[9,16,16]{2,1,0:T(8,128)(2,1)}, u32[]{:S(2)}) copy-start(bf16[9,16,16]{2,1,0:T(8,128)(2,1)} %k2_ref.1) | copy-start | bytes 13828
  3.2 0.7 %copy-start.3 = (f32[16,9]{1,0:T(8,128)S(1)}, f32[16,9]{1,0:T(8,128)}, u32[]{:S(2)}) copy-start(f32[16,9]{1,0:T(8,128)} %k1_ref.1) | copy-start | bytes 1732

commit v2 on v1

--- a/solution.py
+++ b/solution.py
@@ -17,6 +17,7 @@
 F32 = jnp.float32
 BF16 = jnp.bfloat16
 MESH = pl.DeviceIdType.MESH
+SHIFT = jnp.bfloat16
 STEPS = [(-1, 0), (1, 0), (0, -1), (0, 1), (-1, -1), (-1, 1), (1, -1), (1, 1)]
 
 
@@ -25,7 +26,7 @@
     phase = (positions[:, None] * positions[None, :]) % PATCH
     angles = phase * (2.0 * math.pi / PATCH)
     both = np.concatenate([np.cos(angles), np.sin(angles)], axis=1) / math.sqrt(PATCH)
-    return both.astype(np.float32).astype(jnp.bfloat16)
+    return both.astype(np.float32)
 
 
 def iota(shape, dim):
@@ -116,14 +117,23 @@
 
 def body(
     sizes,
+    x_hbm, k1_hbm, k2_hbm, table_hbm, b1_hbm, b2_hbm, hw_hbm,
+    out_ref,
     x_ref, k1_ref, k2_ref, table_ref, b1_ref, b2_ref, hw_ref,
-    out_ref,
     halo, shifted, hidden, own, following, w1_ref, w2_ref,
-    halo_send, halo_recv, next_send, next_recv,
+    halo_send, halo_recv, next_send, next_recv, local_sem,
 ):
     n_gz, n_gy, n_gx = sizes
     height, width = x_ref.shape
     wide = width + LANES
+    near = [k1_ref, b1_ref, k2_ref, b2_ref, x_ref, hw_ref, table_ref]
+    far = [k1_hbm, b1_hbm, k2_hbm, b2_hbm, x_hbm, hw_hbm, table_hbm]
+    loads = [
+        pltpu.make_async_copy(source, target, local_sem.at[n])
+        for n, (source, target) in enumerate(zip(far, near))
+    ]
+    for load in loads:
+        load.start()
     gz, gy, gx = lax.axis_index("gz"), lax.axis_index("gy"), lax.axis_index("gx")
 
     def present(dy, dx):
@@ -167,7 +177,7 @@
         (r0, rn), (c0, cn) = row_src[dy], col_src[dx]
         copies.append(
             pltpu.make_async_remote_copy(
-                src_ref=x_ref.at[pl.ds(r0, rn), pl.ds(c0, cn)],
+                src_ref=x_hbm.at[pl.ds(r0, rn), pl.ds(c0, cn)],
                 dst_ref=halo.at[pl.ds(row_dst[dy], rn), pl.ds(col_dst[dx], cn)],
                 send_sem=halo_send.at[n],
                 recv_sem=halo_recv.at[n],
@@ -186,8 +196,14 @@
             rn, cn = row_src[dy][1], col_src[dx][1]
             halo[pl.ds(row_dst[dy], rn), pl.ds(col_dst[dx], cn)] = jnp.zeros((rn, cn), BF16)
 
+    loads[0].wait()
+    loads[1].wait()
     w1_ref[...] = first_weights(k1_ref, b1_ref)
+    loads[2].wait()
+    loads[3].wait()
     w2_ref[...] = second_weights(k2_ref, b2_ref)
+    for load in loads[4:]:
+        load.wait()
 
     for n, (dy, dx) in enumerate(STEPS):
 
@@ -195,49 +211,58 @@
         def _():
             copies[n].wait_recv()
 
+    def shift(blocks, step, before, after):
+        lane = iota(blocks[0].shape, 1)
+        rolled = [pltpu.roll(block, step % LANES, 1) for block in blocks]
+        if step > 0:
+            fill = [before] + rolled[:-1]
+            return [jnp.where(lane == 0, f, r) for f, r in zip(fill, rolled)]
+        fill = rolled[1:] + [after]
+        return [jnp.where(lane == LANES - 1, f, r) for f, r in zip(fill, rolled)]
+
     def place(row, size, centre):
-        right = halo[pl.ds(row, size), pl.ds(width, LANES)].astype(F32)
-        left = halo[pl.ds(row, size), pl.ds(width + LANES, LANES)].astype(F32)
-        side = jnp.where(iota((size, LANES), 1) < LANES // 2, right, left)
-        ring = jnp.concatenate([centre.astype(F32), side], axis=1)
-        shifted[0, pl.ds(row, size), :] = pltpu.roll(ring, 1, 1).astype(BF16)
-        shifted[1, pl.ds(row, size), :] = ring.astype(BF16)
-        shifted[2, pl.ds(row, size), :] = pltpu.roll(ring, wide - 1, 1).astype(BF16)
+        lane = iota((size, LANES), 1)
+        right = halo[row : row + size, width : width + LANES].astype(F32)
+        left = halo[row : row + size, width + LANES : width + 2 * LANES].astype(F32)
+        blocks = [centre[:, n : n + LANES].astype(F32) for n in range(0, width, LANES)]
+        left_1, right_1 = pltpu.roll(left, 1, 1), pltpu.roll(right, LANES - 1, 1)
+        taps = [
+            shift(blocks, 1, left_1, None)
+            + [jnp.where(lane == LANES - 1, blocks[-1], pltpu.roll(left, 2, 1))],
+            blocks + [jnp.where(lane == LANES - 1, right_1, left_1)],
+            shift(blocks, -1, None, right_1)
+            + [jnp.where(lane == LANES - 1, pltpu.roll(right, LANES - 2, 1), blocks[0])],
+        ]
+        for b in range(3):
+            shifted[b, row : row + size, :] = jnp.concatenate(taps[b], axis=1).astype(BF16)
 
     place(0, EDGE, halo[0:EDGE, 0:width])
+    for row in range(0, height, 64):
+        place(EDGE + row, 64, x_ref[row : row + 64, :])
     place(EDGE + height, EDGE, halo[EDGE + height : 2 * EDGE + height, 0:width])
 
-    def fill(i, carry):
-        place(EDGE + i * 64, 64, x_ref[pl.ds(pl.multiple_of(i * 64, 64), 64), :])
-        return carry
-
-    lax.fori_loop(0, height // 64, fill, 0)
-
-    lane = iota((1, wide), 1)
-    keep = (lane < width) | ((lane == width) & (gx < n_gx - 1)) | ((lane == wide - 1) & (gx > 0))
+    lane = iota((1, LANES), 1)
+    keep = ((lane == 0) & (gx > 0)) | ((lane == LANES - 1) & (gx < n_gx - 1))
     keep = jnp.where(keep, 1.0, 0.0)
 
     def layer_one(i, rows):
-        start = pl.multiple_of(i * 16, 16)
-        taps = [shifted[b, pl.ds(start, 32), :] for b in range(3)]
+        start = i * 16
+        taps = [shifted[b, start : start + 32, :] for b in range(3)]
         stack = jnp.concatenate(taps + taps + [jnp.ones((16, wide), BF16)], axis=0)
-        value = dot(w1_ref[0 : rows * CH, 0:208], stack)
-        value = jnp.maximum(value, 0.0) * keep
-        hidden[pl.ds(start, rows), CH : 2 * CH, :] = (
-            value[:, :width].astype(BF16).reshape(rows, CH, width)
-        )
-        hidden[pl.ds(start, rows), 0:CH, :] = (
-            pltpu.roll(value, 1, 1)[:, :width].astype(BF16).reshape(rows, CH, width)
-        )
-        hidden[pl.ds(start, rows), 2 * CH : 3 * CH, :] = (
-            pltpu.roll(value, wide - 1, 1)[:, :width].astype(BF16).reshape(rows, CH, width)
-        )
+        value = jnp.maximum(dot(w1_ref[0 : rows * CH, 0:208], stack), 0.0)
+        outer = (value[:, width:] * keep).astype(SHIFT)
+        blocks = [value[:, n : n + LANES].astype(SHIFT) for n in range(0, width, LANES)]
+        for b, part in enumerate([shift(blocks, 1, outer, None), blocks, shift(blocks, -1, None, outer)]):
+            hidden[start : start + rows, b * CH : (b + 1) * CH, :] = (
+                jnp.concatenate(part, axis=1).astype(BF16).reshape(rows, CH, width)
+            )
 
     def layer_two(i):
-        start = pl.multiple_of(i * 16, 16)
+        start = i * 16
         rows = []
         for g in range(2):
-            window = hidden[pl.ds(start + g * ROWS_OUT, ROWS_OUT + 2), :, :].reshape(480, width)
+            first = start + g * ROWS_OUT
+            window = hidden[first : first + ROWS_OUT + 2, :, :].reshape(480, width)
             stack = jnp.concatenate([window, jnp.ones((16, width), BF16)], axis=0)
             deep = jnp.maximum(dot(w2_ref[:, 0:496], stack), 0.0)
             total = hw_ref[0] * deep[0:ROWS_OUT]
@@ -245,16 +270,7 @@
                 total = total + hw_ref[o] * deep[o * ROWS_OUT : (o + 1) * ROWS_OUT]
             rows.append(total)
         total = jnp.concatenate(rows, axis=0)
-        centre = x_ref[pl.ds(start, 16), :].astype(F32)
-        own[pl.ds(start, 16), :] = (centre + total).astype(BF16)
-
-    def one(i, carry):
-        layer_one(i, 16)
-        return carry
-
-    def two(i, carry):
-        layer_two(i)
-        return carry
+        own[start : start + 16, :] = (x_ref[start : start + 16, :].astype(F32) + total).astype(BF16)
 
     bands = height // PATCH
     per_band = PATCH // 16
@@ -263,7 +279,8 @@
     done = 0
     for band in range(bands):
         upto = min((band + 1) * per_band + 1, blocks)
-        lax.fori_loop(done, upto, one, 0)
+        for i in range(done, upto):
+            layer_one(i, 16)
         done = upto
         if band == 0:
 
@@ -278,7 +295,8 @@
             def _():
                 hidden[height + 1, :, :] = jnp.zeros((3 * CH, width), BF16)
 
-        lax.fori_loop(band * per_band, (band + 1) * per_band, two, 0)
+        for i in range(band * per_band, (band + 1) * per_band):
+            layer_two(i)
         sends.append(
             pltpu.make_async_remote_copy(
                 src_ref=own.at[pl.ds(band * PATCH, PATCH), :],
@@ -296,7 +314,7 @@
 
     @pl.when(not_last)
     def _():
-        table = table_ref[...]
+        table = table_ref[...].astype(BF16)
         spectra = [spectrum(own[band * PATCH : (band + 1) * PATCH, :], table) for band in range(bands)]
         for band in range(bands):
             sends[band].wait_recv()
@@ -326,13 +344,20 @@
     height, width = section.shape[1:]
     bands = height // PATCH
     vmem = pl.BlockSpec(memory_space=pltpu.VMEM)
-    smem = pl.BlockSpec(memory_space=pltpu.SMEM)
+    hbm = pl.BlockSpec(memory_space=pltpu.HBM)
     return pl.pallas_call(
         functools.partial(body, sizes),
         out_shape=jax.ShapeDtypeStruct((1, 2, height, width), F32),
-        in_specs=[vmem] * 4 + [smem] * 3,
+        in_specs=[hbm] * 7,
         out_specs=vmem,
         scratch_shapes=[
+            pltpu.VMEM((height, width), BF16),
+            pltpu.VMEM(first_kernel.shape, F32),
+            pltpu.VMEM(second_kernel.shape, BF16),
+            pltpu.VMEM((PATCH, 2 * PATCH), F32),
+            pltpu.SMEM((CH,), F32),
+            pltpu.SMEM((CH,), F32),
+            pltpu.SMEM((CH,), F32),
             pltpu.VMEM((height + 2 * EDGE, width + 2 * LANES), BF16),
             pltpu.VMEM((3, height + 2 * EDGE, width + LANES), BF16),
             pltpu.VMEM((height + 16, 3 * CH, width), BF16),
@@ -344,6 +369,7 @@
             pltpu.SemaphoreType.DMA((8,)),
             pltpu.SemaphoreType.DMA((bands,)),
             pltpu.SemaphoreType.DMA((bands,)),
+            pltpu.SemaphoreType.DMA((7,)),
         ],
         compiler_params=pltpu.CompilerParams(
             collective_id=0, has_side_effects=True, vmem_limit_bytes=48 * 1024 * 1024

time: 26.1 us -> 19.3 us (0.74)
  Pallas kernels: 21.1 us -> 14.2 us
    pallas_call x1, Pallas kernels: 21.1 us -> 14.2 us  [on_device(): pl.pallas_call(functools.partial(body, sizes), out_shape=jax.ShapeDtypeSt...]
where the time goes in v2:
time: 19.3 us; the launch traced here: 19 us
  Pallas kernels  14.2 us (74%)
  local copies, waits for them, and re-layouts  4.75 us (25%)
    pallas_call x1, Pallas kernels, on_device(): pl.pallas_call(functools.partial(body, sizes), out_shape=jax.ShapeDtypeSt...  14.2 us
    unnamed x15, local copies, waits for them, and re-layouts  4.75 us

profile of v2, /device:TPU:0, one launch (start us, length us, event | category | flops | bytes accessed | tf_op | source)
XLA Modules:
  0.0 19.0 jit_solution(8578120280663219565)
XLA Ops:
  0.0 0.0 copy-start.6
  0.0 0.0 copy-start.5
  0.0 0.0 copy-start.4
  0.0 0.6 %copy-done.6 = f32[16]{0:T(128)S(1)} copy-done((f32[16]{0:T(128)S(1)}, f32[16]{0:T(128)}, u32[]{:S(2)}) %copy-start.6) | copy-done | bytes 88
  0.7 0.0 copy-done.5
  0.7 0.0 copy-done.4
  0.7 0.0 copy-start
  0.7 0.9 %copy-done = bf16[1,256,256]{2,1,0:T(8,128)(2,1)S(1)} copy-done((bf16[1,256,256]{2,1,0:T(8,128)(2,1)S(1)}, bf16[1,256,256]{2,1,0:T(8,128)(2,1)}, u32[]{:S(2)}) %copy-start) | copy-done | bytes 131096
  1.6 0.0 copy-start.1
  1.6 0.9 %copy-done.1 = f32[128,256]{1,0:T(8,128)S(1)} copy-done((f32[128,256]{1,0:T(8,128)S(1)}, f32[128,256]{1,0:T(8,128)}, u32[]{:S(2)}) %copy-start.1) | copy-done | bytes 131096
  2.5 0.0 copy-start.2
  2.5 0.8 %copy-done.2 = bf16[9,16,16]{2,1,0:T(8,128)(2,1)S(1)} copy-done((bf16[9,16,16]{2,1,0:T(8,128)(2,1)S(1)}, bf16[9,16,16]{2,1,0:T(8,128)(2,1)}, u32[]{:S(2)}) %copy-start.2) | copy-done | bytes 4632
  3.3 0.0 copy-start.3
  3.3 0.7 %copy-done.3 = f32[16,9]{1,0:T(8,128)S(1)} copy-done((f32[16,9]{1,0:T(8,128)S(1)}, f32[16,9]{1,0:T(8,128)}, u32[]{:S(2)}) %copy-start.3) | copy-done | bytes 600
  4.0 14.2 %restore_spectra.1 = f32[1,2,256,256]{3,2,1,0:T(8,128)S(1)} custom-call(bf16[256,256]{1,0:T(8,128)(2,1)S(1)} %bitcast.1, f32[16,9]{1,0:T(8,128)S(1)} %copy-done.3, bf16[9,16,16]{2,1,0:T(8,128)(2,1)S(1)} %copy-done.2, f32[128,256]{1,0:T(8,128)S(1)} %copy-done.1, f32[16]{0:T(128)S(1)} %copy-done.4, f32[16]{0:T(128)S(1)} %copy-done.5, f32[16]{0:T(128)S(1)} %copy-done.6), custom_call_target="tpu_custom_call" | custom-call | tf_op jit(solution)/shard_map/restore_spectra/pallas_call | solution.py:348
  18.2 0.8 %copy.9 = f32[1,2,256,256]{3,2,1,0:T(8,128)} copy(f32[1,2,256,256]{3,2,1,0:T(8,128)S(1)} %restore_spectra.1) | data formatting | bytes 1048576
Async XLA Ops:
  0.0 0.7 %copy-start.6 = (f32[16]{0:T(128)S(1)}, f32[16]{0:T(128)}, u32[]{:S(2)}) copy-start(f32[16]{0:T(128)} %hw_hbm.1) | copy-start | bytes 196
  0.0 0.7 %copy-start.5 = (f32[16]{0:T(128)S(1)}, f32[16]{0:T(128)}, u32[]{:S(2)}) copy-start(f32[16]{0:T(128)} %b2_hbm.1) | copy-start | bytes 196
  0.0 0.7 %copy-start.4 = (f32[16]{0:T(128)S(1)}, f32[16]{0:T(128)}, u32[]{:S(2)}) copy-start(f32[16]{0:T(128)} %b1_hbm.1) | copy-start | bytes 196
  0.7 0.9 %copy-start = (bf16[1,256,256]{2,1,0:T(8,128)(2,1)S(1)}, bf16[1,256,256]{2,1,0:T(8,128)(2,1)}, u32[]{:S(2)}) copy-start(bf16[1,256,256]{2,1,0:T(8,128)(2,1)} %param.7) | copy-start | bytes 393220
  1.6 0.9 %copy-start.1 = (f32[128,256]{1,0:T(8,128)S(1)}, f32[128,256]{1,0:T(8,128)}, u32[]{:S(2)}) copy-start(f32[128,256]{1,0:T(8,128)} %constant.2.clone.table_hbm) | copy-start | bytes 393220
  2.5 0.8 %copy-start.2 = (bf16[9,16,16]{2,1,0:T(8,128)(2,1)S(1)}, bf16[9,16,16]{2,1,0:T(8,128)(2,1)}, u32[]{:S(2)}) copy-start(bf16[9,16,16]{2,1,0:T(8,128)(2,1)} %k2_hbm.1) | copy-start | bytes 13828
  3.3 0.7 %copy-start.3 = (f32[16,9]{1,0:T(8,128)S(1)}, f32[16,9]{1,0:T(8,128)}, u32[]{:S(2)}) copy-start(f32[16,9]{1,0:T(8,128)} %k1_hbm.1) | copy-start | bytes 1732

commit v3 on v2

--- a/solution.py
+++ b/solution.py
@@ -46,11 +46,22 @@
     return out
 
 
-def column_of(ref, ids):
-    column = jnp.zeros(ids.shape, F32)
+def column_of(ref):
+    ids = iota((CH, 1), 0)
+    column = jnp.zeros((CH, 1), F32)
     for c in range(CH):
         column = jnp.where(ids == c, ref[c], column)
     return column
+
+
+def one_hot(hit):
+    return jnp.where(hit, 1.0, 0.0).astype(BF16)
+
+
+def with_bias(values, ref, lanes, first):
+    for n, part in enumerate(pieces(column_of(ref), 3)):
+        values = jnp.where(lanes == first + n, part.astype(F32), values)
+    return values
 
 
 def first_weights(kernel_ref, bias_ref):
@@ -58,41 +69,35 @@
     high, low = pieces(kernel_ref[...], 2)
     k = iota((9, depth), 1)
     tap = iota((9, depth), 0)
-    split, col_off = k // 96, (k % 96) // 32
+    col_off = (k & 127) >> 5
+    lanes = iota((CH, depth), 1)
     m = iota((rows, depth), 0)
     kk = iota((rows, depth), 1)
-    spread = jnp.where(iota((rows, CH), 0) % CH == iota((rows, CH), 1), 1.0, 0.0).astype(BF16)
-    offset = (kk % 96) % 32 - 14 - m // CH
+    spread = one_hot((iota((rows, CH), 0) & (CH - 1)) == iota((rows, CH), 1))
+    fixed = (kk & 127) >= 96
+    offset = (kk & 31) - 14 - (m >> 4)
     weights = jnp.zeros((rows, depth), F32)
     for a in range(3):
-        hit = tap == 3 * a + col_off
-        placed = dot(high, jnp.where(hit & (split == 0), 1.0, 0.0).astype(BF16))
-        placed = placed + dot(low, jnp.where(hit & (split == 1), 1.0, 0.0).astype(BF16))
-        weights = jnp.where(offset == a, dot(spread, placed.astype(BF16)), weights)
-    parts = pieces(column_of(bias_ref, m % CH), 3)
-    weights = jnp.where(kk >= 192, 0.0, weights)
-    for n, part in enumerate(parts):
-        weights = jnp.where(kk == 192 + n, part.astype(F32), weights)
+        hit = (tap == 3 * a + col_off) & (col_off < 3)
+        placed = dot(high, one_hot(hit & (k < 128))) + dot(low, one_hot(hit & (k >= 128)))
+        placed = with_bias(placed, bias_ref, lanes, 96)
+        weights = jnp.where(fixed | (offset == a), dot(spread, placed.astype(BF16)), weights)
     return weights.astype(BF16)
 
 
 def second_weights(kernel_ref, bias_ref):
     rows, depth = ROWS_OUT * CH, 512
     flat = kernel_ref[...].reshape(9 * CH, CH)
-    tile = jnp.where(iota((CH, depth), 1) % CH == iota((CH, depth), 0), 1.0, 0.0).astype(BF16)
-    tiled = dot(flat, tile).astype(BF16)
-    spread = jnp.where(iota((rows, CH), 0) // ROWS_OUT == iota((rows, CH), 1), 1.0, 0.0).astype(BF16)
-    m = iota((rows, depth), 0)
-    kk = iota((rows, depth), 1)
-    slot = kk // CH - 3 * (m % ROWS_OUT)
+    tiled = dot(flat, one_hot((iota((CH, depth), 1) & (CH - 1)) == iota((CH, depth), 0))).astype(BF16)
+    spread = one_hot((iota((rows, CH), 0) >> 3) == iota((rows, CH), 1))
+    slot = (iota((rows, depth), 1) >> 4) - 3 * (iota((rows, depth), 0) & (ROWS_OUT - 1))
     weights = jnp.zeros((rows, depth), F32)
     for t in range(9):
         weights = jnp.where(slot == t, dot(spread, tiled[t * CH : (t + 1) * CH]), weights)
-    parts = pieces(column_of(bias_ref, m // ROWS_OUT), 3)
-    weights = jnp.where(kk >= 480, 0.0, weights)
-    for n, part in enumerate(parts):
-        weights = jnp.where(kk == 480 + n, part.astype(F32), weights)
-    return weights.astype(BF16)
+    lanes = iota((CH, LANES), 1)
+    bias = with_bias(jnp.zeros((CH, LANES), F32), bias_ref, lanes, 96)
+    tail = jnp.where(iota((rows, LANES), 1) >= 96, dot(spread, bias.astype(BF16)), weights[:, 384:])
+    return jnp.concatenate([weights[:, :384], tail], axis=1).astype(BF16)
 
 
 def spectrum(image, table):
@@ -115,13 +120,17 @@
     return both[:PATCH], both[PATCH:]
 
 
+def chunk_bounds(height):
+    return list(range(0, height - PATCH + 1, PATCH)) + [height - PATCH // 2, height - PATCH // 4, height]
+
+
 def body(
     sizes,
     x_hbm, k1_hbm, k2_hbm, table_hbm, b1_hbm, b2_hbm, hw_hbm,
-    out_ref,
+    out_hbm,
     x_ref, k1_ref, k2_ref, table_ref, b1_ref, b2_ref, hw_ref,
     halo, shifted, hidden, own, following, w1_ref, w2_ref,
-    halo_send, halo_recv, next_send, next_recv, local_sem,
+    halo_send, halo_recv, next_send, next_recv, local_sem, out_ref, out_sem,
 ):
     n_gz, n_gy, n_gx = sizes
     height, width = x_ref.shape
@@ -205,11 +214,13 @@
     for load in loads[4:]:
         load.wait()
 
-    for n, (dy, dx) in enumerate(STEPS):
-
-        @pl.when(present(-dy, -dx))
-        def _():
-            copies[n].wait_recv()
+    def receive(chosen):
+        for n in chosen:
+            dy, dx = STEPS[n]
+
+            @pl.when(present(-dy, -dx))
+            def _():
+                copies[n].wait_recv()
 
     def shift(blocks, step, before, after):
         lane = iota(blocks[0].shape, 1)
@@ -222,9 +233,9 @@
 
     def place(row, size, centre):
         lane = iota((size, LANES), 1)
-        right = halo[row : row + size, width : width + LANES].astype(F32)
-        left = halo[row : row + size, width + LANES : width + 2 * LANES].astype(F32)
-        blocks = [centre[:, n : n + LANES].astype(F32) for n in range(0, width, LANES)]
+        right = halo[row : row + size, width : width + LANES]
+        left = halo[row : row + size, width + LANES : width + 2 * LANES]
+        blocks = [centre[:, n : n + LANES] for n in range(0, width, LANES)]
         left_1, right_1 = pltpu.roll(left, 1, 1), pltpu.roll(right, LANES - 1, 1)
         taps = [
             shift(blocks, 1, left_1, None)
@@ -234,22 +245,32 @@
             + [jnp.where(lane == LANES - 1, pltpu.roll(right, LANES - 2, 1), blocks[0])],
         ]
         for b in range(3):
-            shifted[b, row : row + size, :] = jnp.concatenate(taps[b], axis=1).astype(BF16)
-
-    place(0, EDGE, halo[0:EDGE, 0:width])
+            shifted[b, row : row + size, :] = jnp.concatenate(taps[b], axis=1)
+
+    def place_edges():
+        place(0, EDGE, halo[0:EDGE, 0:width])
+        place(EDGE + height, EDGE, halo[EDGE + height : 2 * EDGE + height, 0:width])
+
+    receive((2, 3))
     for row in range(0, height, 64):
         place(EDGE + row, 64, x_ref[row : row + 64, :])
-    place(EDGE + height, EDGE, halo[EDGE + height : 2 * EDGE + height, 0:width])
 
     lane = iota((1, LANES), 1)
     keep = ((lane == 0) & (gx > 0)) | ((lane == LANES - 1) & (gx < n_gx - 1))
     keep = jnp.where(keep, 1.0, 0.0)
+    above = jnp.where(gy > 0, 1.0, 0.0)
+    below = jnp.where(gy < n_gy - 1, 1.0, 0.0)
+    blocks_16 = height // 16
 
     def layer_one(i, rows):
         start = i * 16
         taps = [shifted[b, start : start + 32, :] for b in range(3)]
-        stack = jnp.concatenate(taps + taps + [jnp.ones((16, wide), BF16)], axis=0)
-        value = jnp.maximum(dot(w1_ref[0 : rows * CH, 0:208], stack), 0.0)
+        stack = jnp.concatenate(taps + [jnp.ones((32, wide), BF16)] + taps, axis=0)
+        value = jnp.maximum(dot(w1_ref[0 : rows * CH, 0:224], stack), 0.0)
+        if i == 0:
+            value = jnp.concatenate([value[:CH] * above, value[CH:]], axis=0)
+        if i == blocks_16:
+            value = jnp.concatenate([value[:CH], value[CH : 2 * CH] * below], axis=0)
         outer = (value[:, width:] * keep).astype(SHIFT)
         blocks = [value[:, n : n + LANES].astype(SHIFT) for n in range(0, width, LANES)]
         for b, part in enumerate([shift(blocks, 1, outer, None), blocks, shift(blocks, -1, None, outer)]):
@@ -273,60 +294,69 @@
         own[start : start + 16, :] = (x_ref[start : start + 16, :].astype(F32) + total).astype(BF16)
 
     bands = height // PATCH
-    per_band = PATCH // 16
-    blocks = height // 16
+    bounds = chunk_bounds(height)
     sends = []
-    done = 0
-    for band in range(bands):
-        upto = min((band + 1) * per_band + 1, blocks)
-        for i in range(done, upto):
-            layer_one(i, 16)
-        done = upto
-        if band == 0:
-
-            @pl.when(gy == 0)
-            def _():
-                hidden[0, :, :] = jnp.zeros((3 * CH, width), BF16)
-
-        if band == bands - 1:
-            layer_one(blocks, 2)
-
-            @pl.when(gy == n_gy - 1)
-            def _():
-                hidden[height + 1, :, :] = jnp.zeros((3 * CH, width), BF16)
-
-        for i in range(band * per_band, (band + 1) * per_band):
-            layer_two(i)
+    for n in range(len(bounds) - 1):
+        rows = pl.ds(bounds[n], bounds[n + 1] - bounds[n])
         sends.append(
             pltpu.make_async_remote_copy(
-                src_ref=own.at[pl.ds(band * PATCH, PATCH), :],
-                dst_ref=following.at[pl.ds(band * PATCH, PATCH), :],
-                send_sem=next_send.at[band],
-                recv_sem=next_recv.at[band],
+                src_ref=own.at[rows, :],
+                dst_ref=following.at[rows, :],
+                send_sem=next_send.at[n],
+                recv_sem=next_recv.at[n],
                 device_id=device(-1, 0, 0),
                 device_id_type=MESH,
             )
         )
 
-        @pl.when(not_first)
-        def _():
-            sends[band].start()
+    ahead = 4
+    for i in range(1, ahead):
+        layer_one(i, 16)
+    receive((0, 1, 4, 5, 6, 7))
+    place_edges()
+    layer_one(0, 16)
+    for i in range(blocks_16):
+        j = i + ahead
+        if j < blocks_16:
+            layer_one(j, 16)
+        elif j == blocks_16:
+            layer_one(j, 2)
+        layer_two(i)
+        if (i + 1) * 16 in bounds:
+
+            @pl.when(not_first)
+            def _():
+                sends[bounds.index((i + 1) * 16) - 1].start()
+
+    outs = [
+        pltpu.make_async_copy(
+            out_ref.at[:, pl.ds(band * PATCH, PATCH), :],
+            out_hbm.at[0, :, pl.ds(band * PATCH, PATCH), :],
+            out_sem.at[band],
+        )
+        for band in range(bands)
+    ]
 
     @pl.when(not_last)
     def _():
         table = table_ref[...].astype(BF16)
         spectra = [spectrum(own[band * PATCH : (band + 1) * PATCH, :], table) for band in range(bands)]
         for band in range(bands):
-            sends[band].wait_recv()
+            for n in range(len(sends)):
+                if band * PATCH < bounds[n + 1] <= (band + 1) * PATCH:
+                    sends[n].wait_recv()
             real, imag = spectra[band]
             other_real, other_imag = spectrum(following[band * PATCH : (band + 1) * PATCH, :], table)
             rows = slice(band * PATCH, (band + 1) * PATCH)
-            out_ref[0, 0, rows, :] = real * other_real + imag * other_imag
-            out_ref[0, 1, rows, :] = imag * other_real - real * other_imag
+            out_ref[0, rows, :] = real * other_real + imag * other_imag
+            out_ref[1, rows, :] = imag * other_real - real * other_imag
+            outs[band].start()
 
     @pl.when(jnp.logical_not(not_last))
     def _():
         out_ref[...] = jnp.zeros(out_ref.shape, F32)
+        for out in outs:
+            out.start()
 
     for n, (dy, dx) in enumerate(STEPS):
 
@@ -336,20 +366,23 @@
 
     @pl.when(not_first)
     def _():
-        for band in range(bands):
-            sends[band].wait_send()
+        for send in sends:
+            send.wait_send()
+
+    for out in outs:
+        out.wait()
 
 
 def on_device(sizes, section, first_kernel, first_bias, second_kernel, second_bias, head_weight):
     height, width = section.shape[1:]
     bands = height // PATCH
-    vmem = pl.BlockSpec(memory_space=pltpu.VMEM)
+    chunks = len(chunk_bounds(height)) - 1
     hbm = pl.BlockSpec(memory_space=pltpu.HBM)
     return pl.pallas_call(
         functools.partial(body, sizes),
         out_shape=jax.ShapeDtypeStruct((1, 2, height, width), F32),
         in_specs=[hbm] * 7,
-        out_specs=vmem,
+        out_specs=hbm,
         scratch_shapes=[
             pltpu.VMEM((height, width), BF16),
             pltpu.VMEM(first_kernel.shape, F32),
@@ -367,12 +400,14 @@
             pltpu.VMEM((ROWS_OUT * CH, 512), BF16),
             pltpu.SemaphoreType.DMA((8,)),
             pltpu.SemaphoreType.DMA((8,)),
+            pltpu.SemaphoreType.DMA((chunks,)),
+            pltpu.SemaphoreType.DMA((chunks,)),
+            pltpu.SemaphoreType.DMA((7,)),
+            pltpu.VMEM((2, height, width), F32),
             pltpu.SemaphoreType.DMA((bands,)),
-            pltpu.SemaphoreType.DMA((bands,)),
-            pltpu.SemaphoreType.DMA((7,)),
         ],
         compiler_params=pltpu.CompilerParams(
-            collective_id=0, has_side_effects=True, vmem_limit_bytes=48 * 1024 * 1024
+            collective_id=0, has_side_effects=True, vmem_limit_bytes=64 * 1024 * 1024
         ),
         name="restore_spectra",
     )(section[0], first_kernel, second_kernel, jnp.asarray(dft_table()), first_bias, second_bias, head_weight)

time: 19.3 us -> 16.7 us (0.87)
  local copies, waits for them, and re-layouts: 4.75 us -> 1.87 us
  Pallas kernels: 14.2 us -> 14.6 us
    unnamed x15 -> x1, local copies, waits for them, and re-layouts: 4.75 us -> 1.87 us
    pallas_call x1, Pallas kernels: 14.2 us -> 14.6 us  [on_device(): pl.pallas_call(functools.partial(body, sizes), out_shape=jax.ShapeDtypeSt...]
where the time goes in v3:
time: 16.7 us; the launch traced here: 16.5 us
  Pallas kernels  14.6 us (87%)
  local copies, waits for them, and re-layouts  1.87 us (11%)
    pallas_call x1, Pallas kernels, on_device(): pl.pallas_call(functools.partial(body, sizes), out_shape=jax.ShapeDtypeSt...  14.6 us
    unnamed x1, local copies, waits for them, and re-layouts  1.87 us

profile of v3, /device:TPU:0, one launch (start us, length us, event | category | flops | bytes accessed | tf_op | source)
XLA Modules:
  0.0 16.5 jit_solution(5553111887657690908)
XLA Ops:
  0.0 14.6 %restore_spectra.1 = f32[1,2,256,256]{3,2,1,0:T(8,128)} custom-call(bf16[256,256]{1,0:T(8,128)(2,1)} %bitcast.1, f32[16,9]{1,0:T(8,128)} %k1_hbm.1, bf16[9,16,16]{2,1,0:T(8,128)(2,1)} %k2_hbm.1, f32[128,256]{1,0:T(8,128)} %constant.2.clone.table_hbm, f32[16]{0:T(128)} %b1_hbm.1, f32[16]{0:T(128)} %b2_hbm.1, f32[16]{0:T(128)} %hw_hbm.1), custom_call_target="tpu_custom_call" | custom-call | tf_op jit(solution)/shard_map/restore_spectra/pallas_call | solution.py:381
  14.7 1.9 %copy.9 = f32[1,2,256,256]{3,2,1,0:T(8,128)} copy(f32[1,2,256,256]{3,2,1,0:T(8,128)} %restore_spectra.1) | data formatting | bytes 1048576

commit v4 on v3

--- a/solution.py
+++ b/solution.py
@@ -127,10 +127,10 @@
 def body(
     sizes,
     x_hbm, k1_hbm, k2_hbm, table_hbm, b1_hbm, b2_hbm, hw_hbm,
-    out_hbm,
+    spec_hbm, following,
     x_ref, k1_ref, k2_ref, table_ref, b1_ref, b2_ref, hw_ref,
-    halo, shifted, hidden, own, following, w1_ref, w2_ref,
-    halo_send, halo_recv, next_send, next_recv, local_sem, out_ref, out_sem,
+    halo, shifted, hidden, own, w1_ref, w2_ref,
+    halo_send, halo_recv, next_send, next_recv, local_sem, spec_ref, spec_sem,
 ):
     n_gz, n_gy, n_gx = sizes
     height, width = x_ref.shape
@@ -309,6 +309,16 @@
             )
         )
 
+    stores = [
+        pltpu.make_async_copy(
+            spec_ref.at[:, pl.ds(band * PATCH, PATCH), :],
+            spec_hbm.at[:, pl.ds(band * PATCH, PATCH), :],
+            spec_sem.at[band],
+        )
+        for band in range(bands)
+    ]
+    table = table_ref[...].astype(BF16)
+
     ahead = 4
     for i in range(1, ahead):
         layer_one(i, 16)
@@ -328,26 +338,72 @@
             def _():
                 sends[bounds.index((i + 1) * 16) - 1].start()
 
+        if (i + 1) * 16 % PATCH == 0:
+            band = i * 16 // PATCH
+            rows = slice(band * PATCH, (band + 1) * PATCH)
+            spec_ref[0, rows, :], spec_ref[1, rows, :] = spectrum(own[rows, :], table)
+            stores[band].start()
+
+    for n, (dy, dx) in enumerate(STEPS):
+
+        @pl.when(present(dy, dx))
+        def _():
+            copies[n].wait_send()
+
+    @pl.when(not_first)
+    def _():
+        for send in sends:
+            send.wait_send()
+
+    for store in stores:
+        store.wait()
+
+    @pl.when(not_last)
+    def _():
+        for send in sends:
+            send.wait_recv()
+
+
+def cross_body(
+    n_gz,
+    spec_hbm, following_hbm, table_hbm,
+    out_hbm,
+    spec, following, table_ref, out_ref, sems, out_sems,
+):
+    bands = following.shape[0] // PATCH
+    not_last = lax.axis_index("gz") < n_gz - 1
     outs = [
         pltpu.make_async_copy(
             out_ref.at[:, pl.ds(band * PATCH, PATCH), :],
             out_hbm.at[0, :, pl.ds(band * PATCH, PATCH), :],
-            out_sem.at[band],
+            out_sems.at[band],
         )
         for band in range(bands)
     ]
 
     @pl.when(not_last)
     def _():
+        loads = [pltpu.make_async_copy(table_hbm, table_ref, sems.at[0])]
+        for band in range(bands):
+            rows = pl.ds(band * PATCH, PATCH)
+            loads.append(
+                pltpu.make_async_copy(
+                    following_hbm.at[rows, :], following.at[rows, :], sems.at[1 + 2 * band]
+                )
+            )
+            loads.append(
+                pltpu.make_async_copy(spec_hbm.at[:, rows, :], spec.at[:, rows, :], sems.at[2 + 2 * band])
+            )
+        for load in loads:
+            load.start()
+        loads[0].wait()
         table = table_ref[...].astype(BF16)
-        spectra = [spectrum(own[band * PATCH : (band + 1) * PATCH, :], table) for band in range(bands)]
         for band in range(bands):
-            for n in range(len(sends)):
-                if band * PATCH < bounds[n + 1] <= (band + 1) * PATCH:
-                    sends[n].wait_recv()
-            real, imag = spectra[band]
-            other_real, other_imag = spectrum(following[band * PATCH : (band + 1) * PATCH, :], table)
             rows = slice(band * PATCH, (band + 1) * PATCH)
+            loads[1 + 2 * band].wait()
+            other_real, other_imag = spectrum(following[rows, :], table)
+            loads[2 + 2 * band].wait()
+            real, imag = spec[0, rows, :], spec[1, rows, :]
             out_ref[0, rows, :] = real * other_real + imag * other_imag
             out_ref[1, rows, :] = imag * other_real - real * other_imag
             outs[band].start()
@@ -357,17 +413,6 @@
         out_ref[...] = jnp.zeros(out_ref.shape, F32)
         for out in outs:
             out.start()
-
-    for n, (dy, dx) in enumerate(STEPS):
-
-        @pl.when(present(dy, dx))
-        def _():
-            copies[n].wait_send()
-
-    @pl.when(not_first)
-    def _():
-        for send in sends:
-            send.wait_send()
 
     for out in outs:
         out.wait()
@@ -378,11 +423,15 @@
     bands = height // PATCH
     chunks = len(chunk_bounds(height)) - 1
     hbm = pl.BlockSpec(memory_space=pltpu.HBM)
-    return pl.pallas_call(
+    table = jnp.asarray(dft_table())
+    spec, following = pl.pallas_call(
         functools.partial(body, sizes),
-        out_shape=jax.ShapeDtypeStruct((1, 2, height, width), F32),
+        out_shape=[
+            jax.ShapeDtypeStruct((2, height, width), F32),
+            jax.ShapeDtypeStruct((height, width), BF16),
+        ],
         in_specs=[hbm] * 7,
-        out_specs=hbm,
+        out_specs=[hbm, hbm],
         scratch_shapes=[
             pltpu.VMEM((height, width), BF16),
             pltpu.VMEM(first_kernel.shape, F32),
@@ -394,7 +443,6 @@
             pltpu.VMEM((height + 2 * EDGE, width + 2 * LANES), BF16),
             pltpu.VMEM((3, height + 2 * EDGE, width + LANES), BF16),
             pltpu.VMEM((height + 16, 3 * CH, width), BF16),
-            pltpu.VMEM((height, width), BF16),
             pltpu.VMEM((height, width), BF16),
             pltpu.VMEM((16 * CH, 256), BF16),
             pltpu.VMEM((ROWS_OUT * CH, 512), BF16),
@@ -410,7 +458,23 @@
             collective_id=0, has_side_effects=True, vmem_limit_bytes=64 * 1024 * 1024
         ),
         name="restore_spectra",
-    )(section[0], first_kernel, second_kernel, jnp.asarray(dft_table()), first_bias, second_bias, head_weight)
+    )(section[0], first_kernel, second_kernel, table, first_bias, second_bias, head_weight)
+    return pl.pallas_call(
+        functools.partial(cross_body, sizes[0]),
+        out_shape=jax.ShapeDtypeStruct((1, 2, height, width), F32),
+        in_specs=[hbm] * 3,
+        out_specs=hbm,
+        scratch_shapes=[
+            pltpu.VMEM((2, height, width), F32),
+            pltpu.VMEM((height, width), BF16),
+            pltpu.VMEM((PATCH, 2 * PATCH), F32),
+            pltpu.VMEM((2, height, width), F32),
+            pltpu.SemaphoreType.DMA((1 + 2 * bands,)),
+            pltpu.SemaphoreType.DMA((bands,)),
+        ],
+        compiler_params=pltpu.CompilerParams(vmem_limit_bytes=64 * 1024 * 1024),
+        name="cross_spectra",
+    )(spec, following, table)
 
 
 def solution(mesh):

time: 16.7 us -> 16.4 us (0.982)
  local copies, waits for them, and re-layouts: 1.87 us -> 0 us
  Pallas kernels: 14.6 us -> 16.2 us
    unnamed x1 -> x0, local copies, waits for them, and re-layouts: 1.87 us -> none
    pallas_call x1 -> x2, Pallas kernels: 14.6 us -> 16.2 us  [the longest x1 13.7 us: on_device(): pl.pallas_call(functools.partial(body, sizes), out_shape=[jax.ShapeDtypeS...]
where the time goes in v4:
time: 16.4 us; the launch traced here: 16.2 us
  Pallas kernels  16.2 us (99%)
    pallas_call x1, Pallas kernels, on_device(): pl.pallas_call(functools.partial(body, sizes), out_shape=[jax.ShapeDtypeS...  13.7 us
    pallas_call x1, Pallas kernels, on_device(): pl.pallas_call(functools.partial(cross_body, sizes[0]), out_shape=jax.Sha...  2.56 us

profile of v4, /device:TPU:0, one launch (start us, length us, event | category | flops | bytes accessed | tf_op | source)
XLA Modules:
  0.0 16.2 jit_solution(4143942479193393016)
XLA Ops:
  0.0 13.7 %restore_spectra.1 = (f32[2,256,256]{2,1,0:T(8,128)}, bf16[256,256]{1,0:T(8,128)(2,1)}) custom-call(bf16[256,256]{1,0:T(8,128)(2,1)} %bitcast.1, f32[16,9]{1,0:T(8,128)} %k1_hbm.1, bf16[9,16,16]{2,1,0:T(8,128)(2,1)} %k2_hbm.1, f32[128,256]{1,0:T(8,128)} %constant.2.clone.table_hbm, f32[16]{0:T(128)} %b1_hbm.1, f32[16]{0:T(128)} %b2_hbm.1, f32[16]{0:T(128)} %hw_hbm.1), custom_call_target="tpu_custom_call" | custom-call | tf_op jit(solution)/shard_map/restore_spectra/pallas_call | solution.py:427
  13.7 2.6 %cross_spectra.1 = f32[1,2,256,256]{3,2,1,0:T(8,128)} custom-call(f32[2,256,256]{2,1,0:T(8,128)} %get-tuple-element.7.spec_hbm, bf16[256,256]{1,0:T(8,128)(2,1)} %get-tuple-element.8.following_hbm, f32[128,256]{1,0:T(8,128)} %constant.2.clone.table_hbm), custom_call_target="tpu_custom_call" | custom-call | tf_op jit(solution)/shard_map/cross_spectra/pallas_call | solution.py:462

commit v5 on v3

--- a/solution.py
+++ b/solution.py
@@ -88,16 +88,19 @@
 def second_weights(kernel_ref, bias_ref):
     rows, depth = ROWS_OUT * CH, 512
     flat = kernel_ref[...].reshape(9 * CH, CH)
-    tiled = dot(flat, one_hot((iota((CH, depth), 1) & (CH - 1)) == iota((CH, depth), 0))).astype(BF16)
-    spread = one_hot((iota((rows, CH), 0) >> 3) == iota((rows, CH), 1))
-    slot = (iota((rows, depth), 1) >> 4) - 3 * (iota((rows, depth), 0) & (ROWS_OUT - 1))
-    weights = jnp.zeros((rows, depth), F32)
+    tiled = dot(flat, one_hot((iota((CH, depth), 1) & (CH - 1)) == iota((CH, depth), 0)))
+    tap = iota((CH, depth), 1) >> 4
+    base = jnp.zeros((CH, depth), F32)
     for t in range(9):
-        weights = jnp.where(slot == t, dot(spread, tiled[t * CH : (t + 1) * CH]), weights)
-    lanes = iota((CH, LANES), 1)
-    bias = with_bias(jnp.zeros((CH, LANES), F32), bias_ref, lanes, 96)
-    tail = jnp.where(iota((rows, LANES), 1) >= 96, dot(spread, bias.astype(BF16)), weights[:, 384:])
-    return jnp.concatenate([weights[:, :384], tail], axis=1).astype(BF16)
+        base = jnp.where(tap == t, tiled[t * CH : (t + 1) * CH], base)
+    bias = with_bias(jnp.zeros((CH, depth), F32), bias_ref, iota((CH, depth), 1), 480)
+    shifted = [base + bias]
+    for r in range(1, ROWS_OUT):
+        shifted.append(pltpu.roll(base, 3 * CH * r, 1) + bias)
+    by_row = jnp.concatenate(shifted, axis=0).astype(BF16)
+    m, n = iota((rows, rows), 0), iota((rows, rows), 1)
+    order = one_hot(n == (m & (ROWS_OUT - 1)) * CH + (m >> 3))
+    return dot(order, by_row).astype(BF16)
 
 
 def spectrum(image, table):
@@ -130,7 +133,7 @@
     out_hbm,
     x_ref, k1_ref, k2_ref, table_ref, b1_ref, b2_ref, hw_ref,
     halo, shifted, hidden, own, following, w1_ref, w2_ref,
-    halo_send, halo_recv, next_send, next_recv, local_sem, out_ref, out_sem,
+    halo_send, halo_recv, next_send, next_recv, local_sem, spec_ref, out_ref, out_sem,
 ):
     n_gz, n_gy, n_gx = sizes
     height, width = x_ref.shape
@@ -262,21 +265,37 @@
     below = jnp.where(gy < n_gy - 1, 1.0, 0.0)
     blocks_16 = height // 16
 
-    def layer_one(i, rows):
+    def first_input(i):
         start = i * 16
         taps = [shifted[b, start : start + 32, :] for b in range(3)]
-        stack = jnp.concatenate(taps + [jnp.ones((32, wide), BF16)] + taps, axis=0)
-        value = jnp.maximum(dot(w1_ref[0 : rows * CH, 0:224], stack), 0.0)
+        return jnp.concatenate(taps + [jnp.ones((32, wide), BF16)] + taps, axis=0)
+
+    def first_output(i, rows, value, outer):
+        start = i * 16
+        value, outer = jnp.maximum(value, 0.0), jnp.maximum(outer, 0.0) * keep
         if i == 0:
             value = jnp.concatenate([value[:CH] * above, value[CH:]], axis=0)
+            outer = jnp.concatenate([outer[:CH] * above, outer[CH:]], axis=0)
         if i == blocks_16:
             value = jnp.concatenate([value[:CH], value[CH : 2 * CH] * below], axis=0)
-        outer = (value[:, width:] * keep).astype(SHIFT)
+            outer = jnp.concatenate([outer[:CH], outer[CH : 2 * CH] * below], axis=0)
+        outer = outer.astype(SHIFT)
         blocks = [value[:, n : n + LANES].astype(SHIFT) for n in range(0, width, LANES)]
         for b, part in enumerate([shift(blocks, 1, outer, None), blocks, shift(blocks, -1, None, outer)]):
             hidden[start : start + rows, b * CH : (b + 1) * CH, :] = (
-                jnp.concatenate(part, axis=1).astype(BF16).reshape(rows, CH, width)
+                jnp.concatenate(part, axis=1).reshape(rows, CH, width)
             )
+
+    def layer_one(i, rows):
+        value = dot(w1_ref[0 : rows * CH, 0:224], first_input(i))
+        first_output(i, rows, value[:, :width], value[:, width:])
+
+    def layer_one_pair(i, j):
+        one, two = first_input(i), first_input(j)
+        weights = w1_ref[:, 0:224]
+        outer = dot(weights, jnp.concatenate([one[:, width:], two[:, width:]], axis=1))
+        first_output(i, 16, dot(weights, one[:, :width]), outer[:, :LANES])
+        first_output(j, 16, dot(weights, two[:, :width]), outer[:, LANES:])
 
     def layer_two(i):
         start = i * 16
@@ -309,25 +328,6 @@
             )
         )
 
-    ahead = 4
-    for i in range(1, ahead):
-        layer_one(i, 16)
-    receive((0, 1, 4, 5, 6, 7))
-    place_edges()
-    layer_one(0, 16)
-    for i in range(blocks_16):
-        j = i + ahead
-        if j < blocks_16:
-            layer_one(j, 16)
-        elif j == blocks_16:
-            layer_one(j, 2)
-        layer_two(i)
-        if (i + 1) * 16 in bounds:
-
-            @pl.when(not_first)
-            def _():
-                sends[bounds.index((i + 1) * 16) - 1].start()
-
     outs = [
         pltpu.make_async_copy(
             out_ref.at[:, pl.ds(band * PATCH, PATCH), :],
@@ -336,18 +336,39 @@
         )
         for band in range(bands)
     ]
+    table = table_ref[...].astype(BF16)
+
+    layer_one_pair(1, 2)
+    layer_one_pair(3, 4)
+    receive((0, 1, 4, 5, 6, 7))
+    place_edges()
+    layer_one_pair(0, blocks_16 - 1)
+    for i in range(blocks_16):
+        if i % 2 == 0 and i + 6 < blocks_16 - 1:
+            layer_one_pair(i + 5, i + 6)
+        elif i + 6 == blocks_16 - 1:
+            layer_one(blocks_16, 2)
+        layer_two(i)
+        if (i + 1) * 16 in bounds:
+
+            @pl.when(not_first)
+            def _():
+                sends[bounds.index((i + 1) * 16) - 1].start()
+
+        if (i + 1) * 16 % PATCH == 0:
+            band = i * 16 // PATCH
+            rows = slice(band * PATCH, (band + 1) * PATCH)
+            spec_ref[0, rows, :], spec_ref[1, rows, :] = spectrum(own[rows, :], table)
 
     @pl.when(not_last)
     def _():
-        table = table_ref[...].astype(BF16)
-        spectra = [spectrum(own[band * PATCH : (band + 1) * PATCH, :], table) for band in range(bands)]
         for band in range(bands):
             for n in range(len(sends)):
                 if band * PATCH < bounds[n + 1] <= (band + 1) * PATCH:
                     sends[n].wait_recv()
-            real, imag = spectra[band]
-            other_real, other_imag = spectrum(following[band * PATCH : (band + 1) * PATCH, :], table)
             rows = slice(band * PATCH, (band + 1) * PATCH)
+            other_real, other_imag = spectrum(following[rows, :], table)
+            real, imag = spec_ref[0, rows, :], spec_ref[1, rows, :]
             out_ref[0, rows, :] = real * other_real + imag * other_imag
             out_ref[1, rows, :] = imag * other_real - real * other_imag
             outs[band].start()
@@ -373,12 +394,26 @@
         out.wait()
 
 
+def copy_body(source, target, sems):
+    height = source.shape[2]
+    part = height // 2
+    copies = []
+    for n in range(4):
+        place = (0, n // 2, pl.ds((n % 2) * part, part), slice(None))
+        copies.append(pltpu.make_async_copy(source.at[place], target.at[place], sems.at[n]))
+    for copy in copies:
+        copy.start()
+    for copy in copies:
+        copy.wait()
+
+
 def on_device(sizes, section, first_kernel, first_bias, second_kernel, second_bias, head_weight):
     height, width = section.shape[1:]
     bands = height // PATCH
     chunks = len(chunk_bounds(height)) - 1
     hbm = pl.BlockSpec(memory_space=pltpu.HBM)
-    return pl.pallas_call(
+    table = jnp.asarray(dft_table())
+    product = pl.pallas_call(
         functools.partial(body, sizes),
         out_shape=jax.ShapeDtypeStruct((1, 2, height, width), F32),
         in_specs=[hbm] * 7,
@@ -404,13 +439,23 @@
             pltpu.SemaphoreType.DMA((chunks,)),
             pltpu.SemaphoreType.DMA((7,)),
             pltpu.VMEM((2, height, width), F32),
+            pltpu.VMEM((2, height, width), F32),
             pltpu.SemaphoreType.DMA((bands,)),
         ],
         compiler_params=pltpu.CompilerParams(
             collective_id=0, has_side_effects=True, vmem_limit_bytes=64 * 1024 * 1024
         ),
         name="restore_spectra",
-    )(section[0], first_kernel, second_kernel, jnp.asarray(dft_table()), first_bias, second_bias, head_weight)
+    )(section[0], first_kernel, second_kernel, table, first_bias, second_bias, head_weight)
+    return pl.pallas_call(
+        copy_body,
+        out_shape=jax.ShapeDtypeStruct(product.shape, F32),
+        in_specs=[hbm],
+        out_specs=hbm,
+        scratch_shapes=[pltpu.SemaphoreType.DMA((4,))],
+        compiler_params=pltpu.CompilerParams(vmem_limit_bytes=64 * 1024 * 1024),
+        name="write_result",
+    )(product)
 
 
 def solution(mesh):

time: 16.7 us -> 31.6 us (1.89)
  Pallas kernels: 14.6 us -> 31.5 us
  local copies, waits for them, and re-layouts: 1.87 us -> 0 us
    pallas_call x0 -> x1, Pallas kernels: none -> 17 us  [on_device(): pl.pallas_call(copy_body, out_shape=jax.ShapeDtypeStruct(product.shape, F...]
    unnamed x1 -> x0, local copies, waits for them, and re-layouts: 1.87 us -> none
where the time goes in v5:
time: 31.6 us; the launch traced here: 31.5 us
  Pallas kernels  31.5 us (100%)
    pallas_call x1, Pallas kernels, on_device(): pl.pallas_call(copy_body, out_shape=jax.ShapeDtypeStruct(product.shape, F...  17 us
    pallas_call x1, Pallas kernels, on_device(): pl.pallas_call(functools.partial(body, sizes), out_shape=jax.ShapeDtypeSt...  14.5 us

profile of v5, /device:TPU:0, one launch (start us, length us, event | category | flops | bytes accessed | tf_op | source)
XLA Modules:
  0.0 31.5 jit_solution(7642785699030256512)
XLA Ops:
  0.0 14.5 %restore_spectra.1.source = f32[1,2,256,256]{3,2,1,0:T(8,128)} custom-call(bf16[256,256]{1,0:T(8,128)(2,1)} %bitcast.1, f32[16,9]{1,0:T(8,128)} %k1_hbm.1, bf16[9,16,16]{2,1,0:T(8,128)(2,1)} %k2_hbm.1, f32[128,256]{1,0:T(8,128)} %constant.2.clone.table_hbm, f32[16]{0:T(128)} %b1_hbm.1, f32[16]{0:T(128)} %b2_hbm.1, f32[16]{0:T(128)} %hw_hbm.1), custom_call_target="tpu_custom_call" | custom-call | tf_op jit(solution)/shard_map/restore_spectra/pallas_call | solution.py:416
  14.5 17.0 %write_result.1 = f32[1,2,256,256]{3,2,1,0:T(8,128)} custom-call(f32[1,2,256,256]{3,2,1,0:T(8,128)} %restore_spectra.1.source), custom_call_target="tpu_custom_call" | custom-call | tf_op jit(solution)/shard_map/write_result/pallas_call | solution.py:450

commit v6 on v5

--- a/solution.py
+++ b/solution.py
@@ -124,16 +124,16 @@
 
 
 def chunk_bounds(height):
-    return list(range(0, height - PATCH + 1, PATCH)) + [height - PATCH // 2, height - PATCH // 4, height]
+    return list(range(0, height - 31, 32)) + [height - 16, height]
 
 
 def body(
     sizes,
     x_hbm, k1_hbm, k2_hbm, table_hbm, b1_hbm, b2_hbm, hw_hbm,
-    out_hbm,
+    product_hbm, spec_hbm, tail_hbm,
     x_ref, k1_ref, k2_ref, table_ref, b1_ref, b2_ref, hw_ref,
     halo, shifted, hidden, own, following, w1_ref, w2_ref,
-    halo_send, halo_recv, next_send, next_recv, local_sem, spec_ref, out_ref, out_sem,
+    halo_send, halo_recv, next_send, next_recv, local_sem, spec_ref, product_ref, out_sem,
 ):
     n_gz, n_gy, n_gx = sizes
     height, width = x_ref.shape
@@ -159,10 +159,8 @@
             lax.rem(gx + dx + n_gx, n_gx),
         )
 
-    not_first, not_last = gz > 0, gz < n_gz - 1
-
     barrier = pltpu.get_barrier_semaphore()
-    count = not_first.astype(jnp.int32) + not_last.astype(jnp.int32)
+    count = jnp.int32(2)
     for dy, dx in STEPS:
         count = count + present(dy, dx).astype(jnp.int32)
 
@@ -170,13 +168,8 @@
         def _():
             pl.semaphore_signal(barrier, inc=1, device_id=device(0, dy, dx), device_id_type=MESH)
 
-    @pl.when(not_first)
-    def _():
-        pl.semaphore_signal(barrier, inc=1, device_id=device(-1, 0, 0), device_id_type=MESH)
-
-    @pl.when(not_last)
-    def _():
-        pl.semaphore_signal(barrier, inc=1, device_id=device(1, 0, 0), device_id_type=MESH)
+    for dz in (-1, 1):
+        pl.semaphore_signal(barrier, inc=1, device_id=device(dz, 0, 0), device_id_type=MESH)
 
     pl.semaphore_wait(barrier, count)
 
@@ -317,10 +310,14 @@
     sends = []
     for n in range(len(bounds) - 1):
         rows = pl.ds(bounds[n], bounds[n + 1] - bounds[n])
+        if bounds[n + 1] <= height - PATCH:
+            target = following.at[rows, :]
+        else:
+            target = tail_hbm.at[pl.ds(bounds[n] - height + PATCH, bounds[n + 1] - bounds[n]), :]
         sends.append(
             pltpu.make_async_remote_copy(
                 src_ref=own.at[rows, :],
-                dst_ref=following.at[rows, :],
+                dst_ref=target,
                 send_sem=next_send.at[n],
                 recv_sem=next_recv.at[n],
                 device_id=device(-1, 0, 0),
@@ -328,13 +325,10 @@
             )
         )
 
+    early = height - PATCH
     outs = [
-        pltpu.make_async_copy(
-            out_ref.at[:, pl.ds(band * PATCH, PATCH), :],
-            out_hbm.at[0, :, pl.ds(band * PATCH, PATCH), :],
-            out_sem.at[band],
-        )
-        for band in range(bands)
+        pltpu.make_async_copy(product_ref, product_hbm, out_sem.at[0]),
+        pltpu.make_async_copy(spec_ref.at[:, pl.ds(early, PATCH), :], spec_hbm, out_sem.at[1]),
     ]
     table = table_ref[...].astype(BF16)
 
@@ -350,28 +344,74 @@
             layer_one(blocks_16, 2)
         layer_two(i)
         if (i + 1) * 16 in bounds:
-
-            @pl.when(not_first)
-            def _():
-                sends[bounds.index((i + 1) * 16) - 1].start()
-
+            sends[bounds.index((i + 1) * 16) - 1].start()
         if (i + 1) * 16 % PATCH == 0:
             band = i * 16 // PATCH
             rows = slice(band * PATCH, (band + 1) * PATCH)
             spec_ref[0, rows, :], spec_ref[1, rows, :] = spectrum(own[rows, :], table)
 
+    outs[1].start()
+    for n in range(len(sends)):
+        if bounds[n + 1] <= early:
+            sends[n].wait_recv()
+    for band in range(bands - 1):
+        rows = slice(band * PATCH, (band + 1) * PATCH)
+        other_real, other_imag = spectrum(following[rows, :], table)
+        real, imag = spec_ref[0, rows, :], spec_ref[1, rows, :]
+        product_ref[0, rows, :] = real * other_real + imag * other_imag
+        product_ref[1, rows, :] = imag * other_real - real * other_imag
+    outs[0].start()
+
+    for n, (dy, dx) in enumerate(STEPS):
+
+        @pl.when(present(dy, dx))
+        def _():
+            copies[n].wait_send()
+
+    for n in range(len(sends)):
+        sends[n].wait_send()
+        if bounds[n + 1] > early:
+            sends[n].wait_recv()
+    for out in outs:
+        out.wait()
+
+
+def cross_body(
+    n_gz,
+    product_hbm, spec_hbm, tail_hbm, table_hbm,
+    out_hbm,
+    spec, tail, table_ref, out_ref, sems, out_sems,
+):
+    early = out_ref.shape[1] - PATCH
+    not_last = lax.axis_index("gz") < n_gz - 1
+    outs = [
+        pltpu.make_async_copy(
+            out_ref.at[:, pl.ds(start, size), :], out_hbm.at[0, :, pl.ds(start, size), :], out_sems.at[n]
+        )
+        for n, (start, size) in enumerate([(0, early), (early, PATCH)])
+    ]
+
     @pl.when(not_last)
     def _():
-        for band in range(bands):
-            for n in range(len(sends)):
-                if band * PATCH < bounds[n + 1] <= (band + 1) * PATCH:
-                    sends[n].wait_recv()
-            rows = slice(band * PATCH, (band + 1) * PATCH)
-            other_real, other_imag = spectrum(following[rows, :], table)
-            real, imag = spec_ref[0, rows, :], spec_ref[1, rows, :]
-            out_ref[0, rows, :] = real * other_real + imag * other_imag
-            out_ref[1, rows, :] = imag * other_real - real * other_imag
-            outs[band].start()
+        targets = [table_ref, tail, spec, out_ref.at[:, pl.ds(0, early), :]]
+        sources = [table_hbm, tail_hbm, spec_hbm, product_hbm]
+        loads = [
+            pltpu.make_async_copy(source, target, sems.at[n])
+            for n, (source, target) in enumerate(zip(sources, targets))
+        ]
+        for load in loads:
+            load.start()
+        loads[0].wait()
+        table = table_ref[...].astype(BF16)
+        loads[1].wait()
+        other_real, other_imag = spectrum(tail[...], table)
+        loads[2].wait()
+        real, imag = spec[0], spec[1]
+        out_ref[0, early:, :] = real * other_real + imag * other_imag
+        out_ref[1, early:, :] = imag * other_real - real * other_imag
+        outs[1].start()
+        loads[3].wait()
+        outs[0].start()
 
     @pl.when(jnp.logical_not(not_last))
     def _():
@@ -379,45 +419,25 @@
         for out in outs:
             out.start()
 
-    for n, (dy, dx) in enumerate(STEPS):
-
-        @pl.when(present(dy, dx))
-        def _():
-            copies[n].wait_send()
-
-    @pl.when(not_first)
-    def _():
-        for send in sends:
-            send.wait_send()
-
     for out in outs:
         out.wait()
 
 
-def copy_body(source, target, sems):
-    height = source.shape[2]
-    part = height // 2
-    copies = []
-    for n in range(4):
-        place = (0, n // 2, pl.ds((n % 2) * part, part), slice(None))
-        copies.append(pltpu.make_async_copy(source.at[place], target.at[place], sems.at[n]))
-    for copy in copies:
-        copy.start()
-    for copy in copies:
-        copy.wait()
-
-
 def on_device(sizes, section, first_kernel, first_bias, second_kernel, second_bias, head_weight):
     height, width = section.shape[1:]
-    bands = height // PATCH
     chunks = len(chunk_bounds(height)) - 1
     hbm = pl.BlockSpec(memory_space=pltpu.HBM)
     table = jnp.asarray(dft_table())
-    product = pl.pallas_call(
+    early = height - PATCH
+    product, spec, tail = pl.pallas_call(
         functools.partial(body, sizes),
-        out_shape=jax.ShapeDtypeStruct((1, 2, height, width), F32),
+        out_shape=[
+            jax.ShapeDtypeStruct((2, early, width), F32),
+            jax.ShapeDtypeStruct((2, PATCH, width), F32),
+            jax.ShapeDtypeStruct((PATCH, width), BF16),
+        ],
         in_specs=[hbm] * 7,
-        out_specs=hbm,
+        out_specs=[hbm] * 3,
         scratch_shapes=[
             pltpu.VMEM((height, width), BF16),
             pltpu.VMEM(first_kernel.shape, F32),
@@ -430,7 +450,7 @@
             pltpu.VMEM((3, height + 2 * EDGE, width + LANES), BF16),
             pltpu.VMEM((height + 16, 3 * CH, width), BF16),
             pltpu.VMEM((height, width), BF16),
-            pltpu.VMEM((height, width), BF16),
+            pltpu.VMEM((early, width), BF16),
             pltpu.VMEM((16 * CH, 256), BF16),
             pltpu.VMEM((ROWS_OUT * CH, 512), BF16),
             pltpu.SemaphoreType.DMA((8,)),
@@ -439,8 +459,8 @@
             pltpu.SemaphoreType.DMA((chunks,)),
             pltpu.SemaphoreType.DMA((7,)),
             pltpu.VMEM((2, height, width), F32),
-            pltpu.VMEM((2, height, width), F32),
-            pltpu.SemaphoreType.DMA((bands,)),
+            pltpu.VMEM((2, early, width), F32),
+            pltpu.SemaphoreType.DMA((2,)),
         ],
         compiler_params=pltpu.CompilerParams(
             collective_id=0, has_side_effects=True, vmem_limit_bytes=64 * 1024 * 1024
@@ -448,14 +468,21 @@
         name="restore_spectra",
     )(section[0], first_kernel, second_kernel, table, first_bias, second_bias, head_weight)
     return pl.pallas_call(
-        copy_body,
-        out_shape=jax.ShapeDtypeStruct(product.shape, F32),
-        in_specs=[hbm],
+        functools.partial(cross_body, sizes[0]),
+        out_shape=jax.ShapeDtypeStruct((1, 2, height, width), F32),
+        in_specs=[hbm] * 4,
         out_specs=hbm,
-        scratch_shapes=[pltpu.SemaphoreType.DMA((4,))],
+        scratch_shapes=[
+            pltpu.VMEM((2, PATCH, width), F32),
+            pltpu.VMEM((PATCH, width), BF16),
+            pltpu.VMEM((PATCH, 2 * PATCH), F32),
+            pltpu.VMEM((2, height, width), F32),
+            pltpu.SemaphoreType.DMA((4,)),
+            pltpu.SemaphoreType.DMA((2,)),
+        ],
         compiler_params=pltpu.CompilerParams(vmem_limit_bytes=64 * 1024 * 1024),
-        name="write_result",
-    )(product)
+        name="cross_spectra",
+    )(product, spec, tail, table)
 
 
 def solution(mesh):

time: 31.6 us -> 16.1 us (0.51)
  Pallas kernels: 31.5 us -> 15.9 us
    pallas_call x2, Pallas kernels: 31.5 us -> 15.9 us  [the longest x1 13.8 us: on_device(): pl.pallas_call(functools.partial(body, sizes), out_shape=[jax.ShapeDtypeS...]
where the time goes in v6:
time: 16.1 us; the launch traced here: 16 us
  Pallas kernels  15.9 us (99%)
    pallas_call x1, Pallas kernels, on_device(): pl.pallas_call(functools.partial(body, sizes), out_shape=[jax.ShapeDtypeS...  13.8 us
    pallas_call x1, Pallas kernels, on_device(): pl.pallas_call(functools.partial(cross_body, sizes[0]), out_shape=jax.Sha...  2.2 us

profile of v6, /device:TPU:0, one launch (start us, length us, event | category | flops | bytes accessed | tf_op | source)
XLA Modules:
  0.0 16.0 jit_solution(8627215573470791124)
XLA Ops:
  0.0 13.8 %restore_spectra.1 = (f32[2,128,256]{2,1,0:T(8,128)}, f32[2,128,256]{2,1,0:T(8,128)}, bf16[128,256]{1,0:T(8,128)(2,1)}) custom-call(bf16[256,256]{1,0:T(8,128)(2,1)} %bitcast.1, f32[16,9]{1,0:T(8,128)} %k1_hbm.1, bf16[9,16,16]{2,1,0:T(8,128)(2,1)} %k2_hbm.1, f32[128,256]{1,0:T(8,128)} %constant.2.clone.table_hbm, f32[16]{0:T(128)} %b1_hbm.1, f32[16]{0:T(128)} %b2_hbm.1, ...), custom_call_target="tpu_custom_call" | custom-call | tf_op jit(solution)/shard_map/restore_spectra/pallas_call | solution.py:432
  13.8 2.2 %cross_spectra.1 = f32[1,2,256,256]{3,2,1,0:T(8,128)} custom-call(f32[2,128,256]{2,1,0:T(8,128)} %get-tuple-element.8.product_hbm, f32[2,128,256]{2,1,0:T(8,128)} %get-tuple-element.9.spec_hbm, bf16[128,256]{1,0:T(8,128)(2,1)} %get-tuple-element.10.tail_hbm, f32[128,256]{1,0:T(8,128)} %constant.2.clone.table_hbm), custom_call_target="tpu_custom_call" | custom-call | tf_op jit(solution)/shard_map/cross_spectra/pallas_call | solution.py:470

commit v7 on v6

--- a/solution.py
+++ b/solution.py
@@ -285,23 +285,28 @@
 
     def layer_one_pair(i, j):
         one, two = first_input(i), first_input(j)
-        weights = w1_ref[:, 0:224]
-        outer = dot(weights, jnp.concatenate([one[:, width:], two[:, width:]], axis=1))
-        first_output(i, 16, dot(weights, one[:, :width]), outer[:, :LANES])
-        first_output(j, 16, dot(weights, two[:, :width]), outer[:, LANES:])
+        stack = jnp.concatenate(
+            [one[:, :width], two[:, :width], one[:, width:], two[:, width:]], axis=1
+        )
+        both = dot(w1_ref[:, 0:224], stack)
+        outer = both[:, 2 * width :]
+        first_output(i, 16, both[:, :width], outer[:, :LANES])
+        first_output(j, 16, both[:, width : 2 * width], outer[:, LANES:])
 
     def layer_two(i):
         start = i * 16
-        rows = []
+        windows = []
         for g in range(2):
             first = start + g * ROWS_OUT
-            window = hidden[first : first + ROWS_OUT + 2, :, :].reshape(480, width)
-            stack = jnp.concatenate([window, jnp.ones((16, width), BF16)], axis=0)
-            deep = jnp.maximum(dot(w2_ref[:, 0:496], stack), 0.0)
-            total = hw_ref[0] * deep[0:ROWS_OUT]
-            for o in range(1, CH):
-                total = total + hw_ref[o] * deep[o * ROWS_OUT : (o + 1) * ROWS_OUT]
-            rows.append(total)
+            windows.append(hidden[first : first + ROWS_OUT + 2, :, :].reshape(480, width))
+        stack = jnp.concatenate(
+            [jnp.concatenate(windows, axis=1), jnp.ones((16, 2 * width), BF16)], axis=0
+        )
+        deep = jnp.maximum(dot(w2_ref[:, 0:496], stack), 0.0)
+        total = hw_ref[0] * deep[0:ROWS_OUT]
+        for o in range(1, CH):
+            total = total + hw_ref[o] * deep[o * ROWS_OUT : (o + 1) * ROWS_OUT]
+        rows = [total[:, :width], total[:, width:]]
         total = jnp.concatenate(rows, axis=0)
         own[start : start + 16, :] = (x_ref[start : start + 16, :].astype(F32) + total).astype(BF16)
 

time: 16.1 us -> 16.1 us (level)
  no operation moved by 1% of the time
where the time goes in v7:
time: 16.1 us; the launch traced here: 16 us
  Pallas kernels  15.9 us (99%)
    pallas_call x1, Pallas kernels, on_device(): pl.pallas_call(functools.partial(body, sizes), out_shape=[jax.ShapeDtypeS...  13.8 us
    pallas_call x1, Pallas kernels, on_device(): pl.pallas_call(functools.partial(cross_body, sizes[0]), out_shape=jax.Sha...  2.2 us

profile of v7, /device:TPU:0, one launch (start us, length us, event | category | flops | bytes accessed | tf_op | source)
XLA Modules:
  0.0 16.0 jit_solution(11040773626777584229)
XLA Ops:
  0.0 13.8 %restore_spectra.1 = (f32[2,128,256]{2,1,0:T(8,128)}, f32[2,128,256]{2,1,0:T(8,128)}, bf16[128,256]{1,0:T(8,128)(2,1)}) custom-call(bf16[256,256]{1,0:T(8,128)(2,1)} %bitcast.1, f32[16,9]{1,0:T(8,128)} %k1_hbm.1, bf16[9,16,16]{2,1,0:T(8,128)(2,1)} %k2_hbm.1, f32[128,256]{1,0:T(8,128)} %constant.2.clone.table_hbm, f32[16]{0:T(128)} %b1_hbm.1, f32[16]{0:T(128)} %b2_hbm.1, ...), custom_call_target="tpu_custom_call" | custom-call | tf_op jit(solution)/shard_map/restore_spectra/pallas_call | solution.py:437
  13.8 2.2 %cross_spectra.1 = f32[1,2,256,256]{3,2,1,0:T(8,128)} custom-call(f32[2,128,256]{2,1,0:T(8,128)} %get-tuple-element.8.product_hbm, f32[2,128,256]{2,1,0:T(8,128)} %get-tuple-element.9.spec_hbm, bf16[128,256]{1,0:T(8,128)(2,1)} %get-tuple-element.10.tail_hbm, f32[128,256]{1,0:T(8,128)} %constant.2.clone.table_hbm), custom_call_target="tpu_custom_call" | custom-call | tf_op jit(solution)/shard_map/cross_spectra/pallas_call | solution.py:475

commit v8 on v6

--- a/solution.py
+++ b/solution.py
@@ -64,9 +64,8 @@
     return values
 
 
-def first_weights(kernel_ref, bias_ref):
+def first_weights(kernel_ref, bias_ref, ready):
     rows, depth = 16 * CH, 256
-    high, low = pieces(kernel_ref[...], 2)
     k = iota((9, depth), 1)
     tap = iota((9, depth), 0)
     col_off = (k & 127) >> 5
@@ -76,16 +75,19 @@
     spread = one_hot((iota((rows, CH), 0) & (CH - 1)) == iota((rows, CH), 1))
     fixed = (kk & 127) >= 96
     offset = (kk & 31) - 14 - (m >> 4)
+    hits = [(tap == 3 * a + col_off) & (col_off < 3) for a in range(3)]
+    places = [(one_hot(hit & (k < 128)), one_hot(hit & (k >= 128))) for hit in hits]
+    ready()
+    high, low = pieces(kernel_ref[...], 2)
     weights = jnp.zeros((rows, depth), F32)
     for a in range(3):
-        hit = (tap == 3 * a + col_off) & (col_off < 3)
-        placed = dot(high, one_hot(hit & (k < 128))) + dot(low, one_hot(hit & (k >= 128)))
+        placed = dot(high, places[a][0]) + dot(low, places[a][1])
         placed = with_bias(placed, bias_ref, lanes, 96)
         weights = jnp.where(fixed | (offset == a), dot(spread, placed.astype(BF16)), weights)
     return weights.astype(BF16)
 
 
-def second_weights(kernel_ref, bias_ref):
+def second_weights(kernel_ref, bias_ref, order):
     rows, depth = ROWS_OUT * CH, 512
     flat = kernel_ref[...].reshape(9 * CH, CH)
     tiled = dot(flat, one_hot((iota((CH, depth), 1) & (CH - 1)) == iota((CH, depth), 0)))
@@ -98,8 +100,6 @@
     for r in range(1, ROWS_OUT):
         shifted.append(pltpu.roll(base, 3 * CH * r, 1) + bias)
     by_row = jnp.concatenate(shifted, axis=0).astype(BF16)
-    m, n = iota((rows, rows), 0), iota((rows, rows), 1)
-    order = one_hot(n == (m & (ROWS_OUT - 1)) * CH + (m >> 3))
     return dot(order, by_row).astype(BF16)
 
 
@@ -201,12 +201,16 @@
             rn, cn = row_src[dy][1], col_src[dx][1]
             halo[pl.ds(row_dst[dy], rn), pl.ds(col_dst[dx], cn)] = jnp.zeros((rn, cn), BF16)
 
-    loads[0].wait()
-    loads[1].wait()
-    w1_ref[...] = first_weights(k1_ref, b1_ref)
-    loads[2].wait()
-    loads[3].wait()
-    w2_ref[...] = second_weights(k2_ref, b2_ref)
+    pair = (ROWS_OUT * CH, ROWS_OUT * CH)
+    m, n = iota(pair, 0), iota(pair, 1)
+    order = one_hot(n == (m & (ROWS_OUT - 1)) * CH + (m >> 3))
+
+    def ready():
+        for load in loads[:4]:
+            load.wait()
+
+    w1_ref[...] = first_weights(k1_ref, b1_ref, ready)
+    w2_ref[...] = second_weights(k2_ref, b2_ref, order)
     for load in loads[4:]:
         load.wait()
 
@@ -386,9 +390,13 @@
     not_last = lax.axis_index("gz") < n_gz - 1
     outs = [
         pltpu.make_async_copy(
-            out_ref.at[:, pl.ds(start, size), :], out_hbm.at[0, :, pl.ds(start, size), :], out_sems.at[n]
+            out_ref.at[plane, pl.ds(start, size), :],
+            out_hbm.at[0, plane, pl.ds(start, size), :],
+            out_sems.at[n],
         )
-        for n, (start, size) in enumerate([(0, early), (early, PATCH)])
+        for n, (plane, start, size) in enumerate(
+            [(0, 0, early), (1, 0, early), (0, early, PATCH), (1, early, PATCH)]
+        )
     ]
 
     @pl.when(not_last)
@@ -407,11 +415,13 @@
         other_real, other_imag = spectrum(tail[...], table)
         loads[2].wait()
         real, imag = spec[0], spec[1]
-        out_ref[0, early:, :] = real * other_real + imag * other_imag
-        out_ref[1, early:, :] = imag * other_real - real * other_imag
-        outs[1].start()
         loads[3].wait()
         outs[0].start()
+        outs[1].start()
+        out_ref[0, early:, :] = real * other_real + imag * other_imag
+        outs[2].start()
+        out_ref[1, early:, :] = imag * other_real - real * other_imag
+        outs[3].start()
 
     @pl.when(jnp.logical_not(not_last))
     def _():
@@ -478,7 +488,7 @@
             pltpu.VMEM((PATCH, 2 * PATCH), F32),
             pltpu.VMEM((2, height, width), F32),
             pltpu.SemaphoreType.DMA((4,)),
-            pltpu.SemaphoreType.DMA((2,)),
+            pltpu.SemaphoreType.DMA((4,)),
         ],
         compiler_params=pltpu.CompilerParams(vmem_limit_bytes=64 * 1024 * 1024),
         name="cross_spectra",

time: 16.1 us -> 16.1 us (level)
  no operation moved by 1% of the time
where the time goes in v8:
time: 16.1 us; the launch traced here: 16 us
  Pallas kernels  15.9 us (99%)
    pallas_call x1, Pallas kernels, on_device(): pl.pallas_call(functools.partial(body, sizes), out_shape=[jax.ShapeDtypeS...  13.8 us
    pallas_call x1, Pallas kernels, on_device(): pl.pallas_call(functools.partial(cross_body, sizes[0]), out_shape=jax.Sha...  2.19 us

profile of v8, /device:TPU:0, one launch (start us, length us, event | category | flops | bytes accessed | tf_op | source)
XLA Modules:
  0.0 16.0 jit_solution(7632097783463421142)
XLA Ops:
  0.0 13.8 %restore_spectra.1 = (f32[2,128,256]{2,1,0:T(8,128)}, f32[2,128,256]{2,1,0:T(8,128)}, bf16[128,256]{1,0:T(8,128)(2,1)}) custom-call(bf16[256,256]{1,0:T(8,128)(2,1)} %bitcast.1, f32[16,9]{1,0:T(8,128)} %k1_hbm.1, bf16[9,16,16]{2,1,0:T(8,128)(2,1)} %k2_hbm.1, f32[128,256]{1,0:T(8,128)} %constant.2.clone.table_hbm, f32[16]{0:T(128)} %b1_hbm.1, f32[16]{0:T(128)} %b2_hbm.1, ...), custom_call_target="tpu_custom_call" | custom-call | tf_op jit(solution)/shard_map/restore_spectra/pallas_call | solution.py:442
  13.8 2.2 %cross_spectra.1 = f32[1,2,256,256]{3,2,1,0:T(8,128)} custom-call(f32[2,128,256]{2,1,0:T(8,128)} %get-tuple-element.8.product_hbm, f32[2,128,256]{2,1,0:T(8,128)} %get-tuple-element.9.spec_hbm, bf16[128,256]{1,0:T(8,128)(2,1)} %get-tuple-element.10.tail_hbm, f32[128,256]{1,0:T(8,128)} %constant.2.clone.table_hbm), custom_call_target="tpu_custom_call" | custom-call | tf_op jit(solution)/shard_map/cross_spectra/pallas_call | solution.py:480
